TPU v7x, 32 devices: a whole 2x2x4 slice. The times are simulated.
32 devices in a mesh: pulse: 4 (over y, core), tile: 8 (over z, x).
Axes of the slice: x: 2, y: 2, z: 4, core: 2. Of those that a mesh axis runs over, the one named last changes fastest.
Arguments:
- echoes: bfloat16 [64, 2, 2, 16384], P(('pulse', 'tile')), may hold values from -6 to 6
- pulse_slope: bfloat16 [64, 2], P(('pulse', 'tile')), may hold values from -0.023925781 to 0.023925781
- pulse_shift: bfloat16 [64, 2], P(('pulse', 'tile')), may hold values from -3.140625 to 3.140625
- footprint: int32 [4, 8, 8], P('pulse'), may hold values from -1 to 15, as said below
- band_start: int32 [256], P('tile'), may hold values from 0 to 13216
- row_phase: float32 [256], P('tile'), may hold values from -1 to 1
Outputs:
- formed_image: float32 [2, 256, 4096], P(None, 'tile', 'pulse')
Inputs may be any that keep to these rules, and one draw needn't show every extreme that they name: footprint[g, t] lists in rising order the numbers of group g's blocks whose echoes reach row strip t, then -1 to the end. It names at most one block of each run of 2 numbers that starts at a multiple of 2. In every group some list has 8 entries.
All inputs are finite; a program needn't handle non-finite values.
Results may differ from a plain program's by a relative error of at most 0.0039.
Values may be sent and summed in bfloat16 or wider, within the bound.
A program may use at most 64 MiB of HBM per device.

v0:
```python
import jax
import jax.numpy as jnp
from jax import lax
from jax.sharding import PartitionSpec as P

NCOL = 4096
PB = 2
ITERS = 2


step_size = 0.5
tv_weight = 0.4
floor_square = 0.25


def padded_2(value, sides, width):
    for axis, dim in sides:
        size, length = (lax.axis_size(axis), value.shape[dim])
        up = [(i, (i + 1) % size) for i in range(size - 1)]
        down = [(j, i) for i, j in up]
        last = lax.slice_in_dim(value, length - width, length, axis=dim)
        leading = lax.slice_in_dim(value, 0, width, axis=dim)
        before = lax.ppermute(last, axis, up)
        after = lax.ppermute(leading, axis, down)
        value = jnp.concatenate([before, value, after], axis=dim)
    return value


def cubic_table():
    columns = jnp.arange(128, dtype=jnp.int32)
    quarter_pos = 3 * columns + 4
    base_tap = quarter_pos // 4
    fraction = (quarter_pos % 4).astype(jnp.float32) / 4.0
    fraction_sq = fraction * fraction
    fraction_cube = fraction_sq * fraction
    weights = [
        (-fraction_cube + 2.0 * fraction_sq - fraction) * 0.5,
        (3.0 * fraction_cube - 5.0 * fraction_sq + 2.0) * 0.5,
        (-3.0 * fraction_cube + 4.0 * fraction_sq + fraction) * 0.5,
        (fraction_cube - fraction_sq) * 0.5,
    ]
    tap_rows = jnp.arange(128, dtype=jnp.int32)[:, None]
    cubic_weights = jnp.zeros((128, 128), jnp.float32)
    for tap_shift, weight in zip(range(-1, 3), weights):
        cubic_weights = cubic_weights + jnp.where(
            tap_rows == (base_tap + tap_shift)[None, :], weight[None, :], 0.0
        )
    return cubic_weights


def block_image(block_echo, block_slope, block_shift, band_start, row_phase, cubic_weights):
    pulses = block_echo.shape[0]
    row_count = band_start.shape[0]
    col_blocks = NCOL // 128
    window_span = 96 * (col_blocks + 1)
    flat_echo = block_echo.reshape(pulses * 2, block_echo.shape[2])
    segments = jax.vmap(
        lambda row_start: lax.dynamic_slice_in_dim(flat_echo, row_start, window_span, axis=1)
    )(band_start)
    leading = segments[..., : 96 * col_blocks].reshape(row_count, pulses * 2, col_blocks, 96)
    trailing = segments[..., 96:].reshape(row_count, pulses * 2, col_blocks, 96)[..., :32]
    windows = jnp.concatenate([leading, trailing], axis=-1)
    windows = (
        jnp.transpose(windows, (0, 2, 1, 3))
        .reshape(row_count, col_blocks, pulses, 2, 128)
        .astype(jnp.float32)
    )
    slopes = block_slope.astype(jnp.float32)
    shifts = block_shift.astype(jnp.float32)
    block_pos = (128 * jnp.arange(col_blocks, dtype=jnp.int32)).astype(jnp.float32)
    angle_grid = (
        shifts[None, None, :] * row_phase[:, None, None]
        + slopes[None, None, :] * block_pos[None, :, None]
    )
    cosine = jnp.cos(angle_grid)[..., None]
    sines = jnp.sin(angle_grid)[..., None]
    real_part = windows[:, :, :, 0]
    imag_part = windows[:, :, :, 1]
    turned_re = real_part * cosine - imag_part * sines
    turned_im = real_part * sines + imag_part * cosine
    turned = (
        jnp.stack([turned_re, turned_im], axis=3)
        .astype(jnp.bfloat16)
        .reshape(row_count * col_blocks, pulses * 256)
    )
    column_pos = jnp.arange(128, dtype=jnp.int32).astype(jnp.float32)
    column_ramp = slopes[:, None] * column_pos[None, :]
    kernel_re = cubic_weights[None] * jnp.cos(column_ramp)[:, None, :]
    kernel_im = cubic_weights[None] * jnp.sin(column_ramp)[:, None, :]
    upper_rows = jnp.concatenate([kernel_re, kernel_im], axis=2)
    bottom = jnp.concatenate([-kernel_im, kernel_re], axis=2)
    kernel = jnp.stack([upper_rows, bottom], axis=1).astype(jnp.bfloat16).reshape(pulses * 256, 256)
    product = jnp.dot(turned, kernel, preferred_element_type=jnp.float32)
    return product.reshape(row_count, col_blocks, 256)


def add_used(
    running, echo_all, slope_all, shift_all, slots, used_count, band_start, row_phase, cubic_weights
):
    slot_count = slots.shape[0]

    def add_pair(pair_index, partial_sum):
        first_slot = slots[2 * pair_index]
        second_slot = slots[jnp.minimum(2 * pair_index + 1, slot_count - 1)]
        second_used = 2 * pair_index + 1 < used_count
        second_echo = jnp.where(second_used, echo_all[second_slot], jnp.zeros_like(echo_all[0]))
        echo_pair = jnp.concatenate([echo_all[first_slot], second_echo], axis=0)
        slope_pair = jnp.concatenate([slope_all[first_slot], slope_all[second_slot]], axis=0)
        shift_pair = jnp.concatenate([shift_all[first_slot], shift_all[second_slot]], axis=0)
        return partial_sum + block_image(
            echo_pair, slope_pair, shift_pair, band_start, row_phase, cubic_weights
        )

    return lax.fori_loop(0, (used_count + 1) // 2, add_pair, running)


def tv_update(field, padded, base_image, row_anchor, col_anchor, grid_rows, grid_cols):
    row_count = field.shape[1]
    col_count = field.shape[2]
    grad_rows = (
        padded[:, 1 : row_count + 2, 0 : col_count + 1]
        - padded[:, 0 : row_count + 1, 0 : col_count + 1]
    )
    grad_cols = (
        padded[:, 0 : row_count + 1, 1 : col_count + 2]
        - padded[:, 0 : row_count + 1, 0 : col_count + 1]
    )
    row_ids = row_anchor - 1 + jnp.arange(row_count + 1, dtype=jnp.int32)
    col_ids = col_anchor - 1 + jnp.arange(col_count + 1, dtype=jnp.int32)
    inside = (row_ids >= 0)[:, None] & (col_ids >= 0)[None, :]
    grad_rows = jnp.where((inside & (row_ids < grid_rows - 1)[:, None])[None], grad_rows, 0.0)
    grad_cols = jnp.where((inside & (col_ids < grid_cols - 1)[None, :])[None], grad_cols, 0.0)
    magnitude = jnp.sqrt(
        jnp.sum(grad_rows * grad_rows + grad_cols * grad_cols, axis=0) + floor_square
    )
    flux_rows = grad_rows / magnitude[None]
    flux_cols = grad_cols / magnitude[None]
    divergence = (
        flux_rows[:, 1:, 1:] - flux_rows[:, :-1, 1:] + flux_cols[:, 1:, 1:] - flux_cols[:, 1:, :-1]
    )
    return field - step_size * (field - base_image - tv_weight * divergence)


def to_image(blocks):
    row_count = blocks.shape[0]
    col_count = blocks.shape[1] * 128
    real_plane = blocks[..., :128].reshape(row_count, col_count)
    imag_plane = blocks[..., 128:].reshape(row_count, col_count)
    return jnp.stack([real_plane, imag_plane])


def body(echoes, pulse_slope, pulse_shift, footprint, band_start, row_phase):
    tile_count = lax.axis_size("tile")
    groups = lax.axis_size("pulse")
    tile_index = lax.axis_index("tile")
    group_index = lax.axis_index("pulse")
    row_count = band_start.shape[0]
    col_blocks = NCOL // 128
    cubic_weights = cubic_table()
    footprints = footprint[0]
    own_list = lax.dynamic_index_in_dim(footprints, tile_index, axis=0, keepdims=False)
    zero_image = jnp.zeros((row_count, col_blocks, 256), jnp.float32)
    piece_echo = lax.all_gather(echoes, "tile", axis=0, tiled=True)
    piece_slope = lax.all_gather(pulse_slope, "tile", axis=0, tiled=True)
    piece_shift = lax.all_gather(pulse_shift, "tile", axis=0, tiled=True)
    piece_count = piece_echo.shape[0]
    positions = jnp.arange(piece_count, dtype=jnp.int32)
    is_used = jnp.any(positions[:, None] == own_list[None, :], axis=1)
    ordering = jnp.argsort(jnp.where(is_used, 0, piece_count) + positions)
    used_total = jnp.sum(is_used.astype(jnp.int32))
    partial_image = add_used(
        zero_image,
        piece_echo,
        piece_slope,
        piece_shift,
        ordering,
        used_total,
        band_start,
        row_phase,
        cubic_weights,
    )
    normalize = float(PB * tile_count * groups) ** (-0.5)
    grid_rows = tile_count * row_count
    row_anchor = tile_index * row_count
    whole = lax.psum(partial_image, "pulse")
    base_image = to_image(whole) * normalize
    field = base_image
    for iteration in range(ITERS):
        padded = padded_2(field, (("tile", 1),), 1)
        padded = jnp.pad(padded, ((0, 0), (0, 0), (1, 1)))
        field = tv_update(field, padded, base_image, row_anchor, 0, grid_rows, NCOL)
    share_width = NCOL // groups
    return lax.dynamic_slice_in_dim(field, group_index * share_width, share_width, axis=2)


def solution(mesh):
    in_specs = (
        P(("pulse", "tile"), None, None, None),
        P(("pulse", "tile"), None),
        P(("pulse", "tile"), None),
        P("pulse", None, None),
        P("tile"),
        P("tile"),
    )
    out_specs = P(None, "tile", "pulse")
    return jax.shard_map(body, mesh=mesh, in_specs=in_specs, out_specs=out_specs, check_vma=False)
```

profile of v0, /device:TPU:0, one launch (start us, length us, event | category | flops | bytes accessed | tf_op | source)
XLA Modules:
  0.0 387.2 jit_solution(2665233629765094138)
XLA Ops:
  7.3 22.3 %all-gather = bf16[8,2,2]{2,1,0:T(2,128)(2,1)S(1)} all-gather(bf16[1,2,2]{2,1,0:T(2,128)(2,1)} %bitcast.74), channel_id=1, replica_groups=mesh['pulse'=4,'tile'=8] {'tile'}, dimensions={0}, use_global_device_ids=true | all-gather | bytes 72 | tf_op jit(solution)/shard_map/all_gather | solution.py:165
  29.6 16.4 %all-gather.1 = bf16[8,2,2]{2,1,0:T(2,128)(2,1)S(1)} all-gather(bf16[1,2,2]{2,1,0:T(2,128)(2,1)} %bitcast.75), channel_id=1, replica_groups=mesh['pulse'=4,'tile'=8] {'tile'}, dimensions={0}, use_global_device_ids=true | all-gather | bytes 72 | tf_op jit(solution)/shard_map/all_gather | solution.py:164
  47.4 1.3 sort.17
  48.8 12.7 %all-gather.4.cloned.1.call-done = bf16[16,2,2,16384]{3,2,1,0:T(2,128)(2,1)} async-done(((bf16[2,2,2,16384]{3,2,1,0:T(2,128)(2,1)}), bf16[16,2,2,16384]{3,2,1,0:T(2,128)(2,1)}) %all-gather.4.cloned.1.call-update) | async-done | bytes 2097168 | tf_op jit(solution)/shard_map/all_gather | solution.py:163
  61.6 127.7 %while.17 = (s32[]{:T(128)}, f32[32,32,256]{2,1,0:T(8,128)S(1)}, s32[]{:T(128)}, s32[16]{0:T(128)S(1)}, bf16[16,2,2,16384]{3,2,1,0:T(2,128)(2,1)}, /*index=5*/s3...) while((s32[]{:T(128)}, f32[32,32,256]{2,1,0:T(8,128)S(1)}, ...), condition=%wide.region_4.5_spmd.clone.clone, body=%wide.region_3.4_spmd.clone.clone.sunk | while | flops 548656192 | bytes 41472712 | solution.py:114
  68.3 40.2 %while.18 = (s32[]{:T(128)}, bf16[8,16384]{1,0:T(8,128)(2,1)S(1)}, s32[32,2]{0,1:T(2,128)S(1)}, bf16[32,8,3168]{2,1,0:T(8,128)(2,1)S(1)}, s32[]{:T(128)}) while((s32[]{:T(128)}, bf16[8,16384]{1,0:T(8,128)(2,1)S(1)}, s32[32,2]{0,1:T(2,128)S(1)}, bf16[32,8,3168]{2,1,0:T(8,128)(2,1)S(1)}, s32[]{:T(128)}) %tuple.94), condition=%wide.while_cond, body=%wide.while_body.sunk | while | flops 2 | bytes 102497 | solution.py:58
  108.5 2.4 fusion.59
  110.9 3.6 reshape.426
  114.5 4.5 %reshape.427 = bf16[32,8,32,96]{3,2,1,0:T(8,128)(2,1)} reshape(bf16[32,8,3072]{2,1,0:T(8,128)(2,1)} %get-tuple-element.511) | data formatting | bytes 3145728 | tf_op jit(solution)/shard_map/while/body/reshape | solution.py:60
  119.0 2.7 maximum_convert_fusion.6
  123.0 1.4 subtract_convert_fusion.2
  132.1 40.2 %while.18 = (s32[]{:T(128)}, bf16[8,16384]{1,0:T(8,128)(2,1)S(1)}, s32[32,2]{0,1:T(2,128)S(1)}, bf16[32,8,3168]{2,1,0:T(8,128)(2,1)S(1)}, s32[]{:T(128)}) while((s32[]{:T(128)}, bf16[8,16384]{1,0:T(8,128)(2,1)S(1)}, s32[32,2]{0,1:T(2,128)S(1)}, bf16[32,8,3168]{2,1,0:T(8,128)(2,1)S(1)}, s32[]{:T(128)}) %tuple.94), condition=%wide.while_cond, body=%wide.while_body.sunk | while | flops 2 | bytes 102497 | solution.py:58
  172.3 2.4 fusion.59
  174.8 3.6 reshape.426
  178.4 4.5 %reshape.427 = bf16[32,8,32,96]{3,2,1,0:T(8,128)(2,1)} reshape(bf16[32,8,3072]{2,1,0:T(8,128)(2,1)} %get-tuple-element.511) | data formatting | bytes 3145728 | tf_op jit(solution)/shard_map/while/body/reshape | solution.py:60
  182.9 2.7 maximum_convert_fusion.6
  186.9 1.4 subtract_convert_fusion.2
  190.4 162.4 %all-reduce.5.cloned.1.call-done = f32[32,32,256]{2,1,0:T(8,128)} async-done(((f32[32,32,256]{2,1,0:T(8,128)}), f32[32,32,256]{2,1,0:T(8,128)}) %all-reduce.5.cloned.1.call-update) | async-done | bytes 1048592 | tf_op jit(solution)/shard_map/psum | solution.py:185
  354.5 3.4 collective-permute-start
  357.9 1.3 collective-permute-start.1
  359.4 4.2 %collective-permute-done.1 = f32[2,1,4096]{2,1,0:T(1,128)S(1)} collective-permute-done((f32[2,1,4096]{2,1,0:T(1,128)S(1)}, f32[2,1,4096]{2,1,0:T(1,128)S(1)}, u32[]{:S(2)}, u32[]{:S(2)}) %collective-permute-start.1) | collective-permute-done | bytes 32800 | tf_op jit(solution)/shard_map/ppermute | solution.py:24
  366.5 4.3 %collective-permute-start.2 = (f32[2,1,4096]{2,1,0:T(1,128)S(1)}, f32[2,1,4096]{2,1,0:T(1,128)S(1)}, u32[]{:S(2)}, u32[]{:S(2)}) collective-permute-start(f32[2,1,4096]{2,1,0:T(1,128)S(1)} %get-tuple-element.320), channel_id=1, source_target_pairs={{0,1},{1,2},{2,3},{3,4},{4,5},{5,6},{6,7},{8,9},{9,10},{10,11},{11... | collective-permute-start | bytes 98312 | tf_op jit(solution)/shard_map/ppermute | solution.py:23
  370.8 1.5 collective-permute-start.3
  372.4 4.2 %collective-permute-done.3 = f32[2,1,4096]{2,1,0:T(1,128)S(1)} collective-permute-done((f32[2,1,4096]{2,1,0:T(1,128)S(1)}, f32[2,1,4096]{2,1,0:T(1,128)S(1)}, u32[]{:S(2)}, u32[]{:S(2)}) %collective-permute-start.3) | collective-permute-done | bytes 32800 | tf_op jit(solution)/shard_map/ppermute | solution.py:24
  (278 shorter events, 99.5 us)
Async XLA Ops:
  6.5 39.6 %copy-start = (s32[1,8,8]{2,1,0:T(8,128)S(1)}, s32[1,8,8]{2,1,0:T(8,128)}, u32[]{:S(2)}) copy-start(s32[1,8,8]{2,1,0:T(8,128)} %param.11) | copy-start | bytes 772
  6.5 55.1 %copy-start.3 = (s32[32]{0:T(128)S(1)}, s32[32]{0:T(128)}, u32[]{:S(2)}) copy-start(s32[32]{0:T(128)} %param.12) | copy-start | bytes 388
  6.5 55.1 %copy-start.2 = (f32[32]{0:T(128)S(1)}, f32[32]{0:T(128)}, u32[]{:S(2)}) copy-start(f32[32]{0:T(128)} %param.13) | copy-start | bytes 388
  6.5 55.0 %all-gather.4.cloned.1.call-start = ((), (), s32[]{:S(2)}) async-start(), calls=%async_computation | async-start | bytes 2359296 | tf_op jit(solution)/shard_map/all_gather | solution.py:163
  7.3 345.6 %all-reduce.5.cloned.1.call-start = ((), (), s32[]{:S(2)}) async-start(), calls=%async_computation.1 | async-start | bytes 2097152 | tf_op jit(solution)/shard_map/psum | solution.py:185
  189.4 1.0 copy-start.1
  354.5 5.0 %collective-permute-start = (f32[2,1,4096]{2,1,0:T(1,128)S(1)}, f32[2,1,4096]{2,1,0:T(1,128)S(1)}, u32[]{:S(2)}, u32[]{:S(2)}) collective-permute-start(f32[2,1,4096]{2,1,0:T(1,128)S(1)} %get-tuple-element.322), channel_id=1, source_target_pairs={{0,1},{1,2},{2,3},{3,4},{4,5},{5,6},{6,7},{8,9},{9,10},{10,11},{11... | collective-permute-start | bytes 98312 | tf_op jit(solution)/shard_map/ppermute | solution.py:23
  357.9 5.8 %collective-permute-start.1 = (f32[2,1,4096]{2,1,0:T(1,128)S(1)}, f32[2,1,4096]{2,1,0:T(1,128)S(1)}, u32[]{:S(2)}, u32[]{:S(2)}) collective-permute-start(f32[2,1,4096]{2,1,0:T(1,128)S(1)} %get-tuple-element.323), channel_id=1, source_target_pairs={{1,0},{2,1},{3,2},{4,3},{5,4},{6,5},{7,6},{9,8},{10,9},{11,10},{12... | collective-permute-start | bytes 98312 | tf_op jit(solution)/shard_map/ppermute | solution.py:24
  366.5 5.9 %collective-permute-start.2 = (f32[2,1,4096]{2,1,0:T(1,128)S(1)}, f32[2,1,4096]{2,1,0:T(1,128)S(1)}, u32[]{:S(2)}, u32[]{:S(2)}) collective-permute-start(f32[2,1,4096]{2,1,0:T(1,128)S(1)} %get-tuple-element.320), channel_id=1, source_target_pairs={{0,1},{1,2},{2,3},{3,4},{4,5},{5,6},{6,7},{8,9},{9,10},{10,11},{11... | collective-permute-start | bytes 98312 | tf_op jit(solution)/shard_map/ppermute | solution.py:23
  370.8 5.8 %collective-permute-start.3 = (f32[2,1,4096]{2,1,0:T(1,128)S(1)}, f32[2,1,4096]{2,1,0:T(1,128)S(1)}, u32[]{:S(2)}, u32[]{:S(2)}) collective-permute-start(f32[2,1,4096]{2,1,0:T(1,128)S(1)} %get-tuple-element.321), channel_id=1, source_target_pairs={{1,0},{2,1},{3,2},{4,3},{5,4},{6,5},{7,6},{9,8},{10,9},{11,10},{12... | collective-permute-start | bytes 98312 | tf_op jit(solution)/shard_map/ppermute | solution.py:24
Sparse Core Ops, SparseCore 0:
  9.5 51.9 all-gather.3
  190.5 162.2 all-reduce.4
where the time goes:
time: 391 us; the launch traced here: 387 us
  waiting for transfers between devices  184 us (47%)
  local copies, waits for them, and re-layouts  106 us (27%)
  blocking collectives  38.8 us (10%)
  other arithmetic  21.5 us (5%)
  between operations  14.2 us (4%)
  starting transfers between devices  10.5 us (3%)
  loops' own time  10 us (3%)
    psum x1, waiting for transfers between devices, body(): whole = lax.psum(partial_image, 'pulse')  162 us
    gather x192, local copies, waits for them, and re-layouts  79.2 us
    all_gather x1, blocking collectives, body(): piece_shift = lax.all_gather(pulse_shift, 'tile', axis=0, tiled=True)  22.3 us
    all_gather x1, blocking collectives, body(): piece_slope = lax.all_gather(pulse_slope, 'tile', axis=0, tiled=True)  16.4 us
    all_gather x1, waiting for transfers between devices, body(): piece_echo = lax.all_gather(echoes, 'tile', axis=0, tiled=True)  12.7 us
    reshape x2, local copies, waits for them, and re-layouts, block_image(): segments[..., :96 * col_blocks]  9.08 us
    another operation x1, loops' own time, add_used(): return lax.fori_loop(0, (used_count + 1) // 2, add_pair, running)  8.89 us
    ppermute x2, waiting for transfers between devices, padded_2(): after = lax.ppermute(leading, axis, down)  8.46 us
  transfers between devices with their start and end apart: 6, of which 5 were waited for; matrix products, arithmetic and copies ran while one was open for 1% of the time, Pallas kernels for 0%

commit v1 on v0

v1 whole, which is shorter than its diff:
```python
import functools

import jax
import jax.numpy as jnp
import numpy as np
from jax import lax
from jax.experimental import pallas as pl
from jax.experimental.pallas import tpu as pltpu
from jax.sharding import PartitionSpec as P

NCOL = 4096
ITERS = 2
KBLOCKS = NCOL // 128
QUADS = KBLOCKS // 4
HALO = ITERS

step_size = 0.5
tv_weight = 0.4
floor_square = 0.25

MESH = pl.DeviceIdType.MESH
F32 = jnp.float32
BF16 = jnp.bfloat16


def interpolation_table():
    columns = np.arange(128)
    position = 3 * columns + 4
    base = position // 4
    f = (position % 4) / 4.0
    weights = [
        (-(f**3) + 2 * f**2 - f) / 2,
        (3 * f**3 - 5 * f**2 + 2) / 2,
        (-3 * f**3 + 4 * f**2 + f) / 2,
        (f**3 - f**2) / 2,
    ]
    table = np.zeros((512, 512), np.float32)
    for q in range(4):
        for shift, weight in zip(range(-1, 3), weights):
            table[96 * q + base + shift, 128 * q + columns] += weight
    return table


def exchange_kernel(n, blocks_ref, params_ref, got_ref, got_params_ref, sends, recvs, local_sem):
    me = lax.axis_index("tile")
    barrier = pltpu.get_barrier_semaphore()
    for d in range(1, n):
        pl.semaphore_signal(
            barrier, inc=1, device_id={"tile": lax.rem(me + d, n)}, device_id_type=MESH
        )
    own = pltpu.make_async_copy(blocks_ref.at[me], got_ref.at[me], local_sem.at[0])
    own_params = pltpu.make_async_copy(params_ref.at[me], got_params_ref.at[me], local_sem.at[1])
    own.start()
    own_params.start()
    pl.semaphore_wait(barrier, n - 1)
    copies = []
    for d in range(1, n):
        target = lax.rem(me + d, n)
        for j, (src, dst) in enumerate(((params_ref, got_params_ref), (blocks_ref, got_ref))):
            copy = pltpu.make_async_remote_copy(
                src_ref=src.at[target],
                dst_ref=dst.at[me],
                send_sem=sends.at[j, d],
                recv_sem=recvs.at[j, d],
                device_id={"tile": target},
                device_id_type=MESH,
            )
            copy.start()
            copies.append(copy)
    own.wait()
    own_params.wait()
    for copy in copies:
        copy.wait()


def exchange(blocks, params):
    n = blocks.shape[0]
    return pl.pallas_call(
        functools.partial(exchange_kernel, n),
        out_shape=(
            jax.ShapeDtypeStruct(blocks.shape, blocks.dtype),
            jax.ShapeDtypeStruct(params.shape, params.dtype),
        ),
        in_specs=[pl.BlockSpec(memory_space=pl.ANY)] * 2,
        out_specs=[pl.BlockSpec(memory_space=pl.ANY)] * 2,
        scratch_shapes=[
            pltpu.SemaphoreType.DMA((2, n)),
            pltpu.SemaphoreType.DMA((2, n)),
            pltpu.SemaphoreType.DMA((2,)),
        ],
        compiler_params=pltpu.CompilerParams(collective_id=0, has_side_effects=True),
    )(blocks, params)


def image_kernel(
    pulses,
    groups,
    used_ref,
    start_ref,
    echo_ref,
    params_ref,
    phase_ref,
    table_ref,
    out_ref,
    wide,
    turned,
    lhs,
    product,
    ramp,
    rowturn,
    acc,
    image,
):
    n = echo_ref.shape[0]
    bins = echo_ref.shape[2]
    rows = phase_ref.shape[0]
    share = KBLOCKS // groups
    scale = float(pulses * n * groups) ** -0.5
    lane = lax.broadcasted_iota(jnp.int32, (8, 128), 1)
    sub = lax.broadcasted_iota(jnp.int32, (8, 128), 0)
    wide[:, bins:, :] = jnp.zeros((2 * pulses, wide.shape[1] - bins, 128), F32)
    acc[...] = jnp.zeros_like(acc)

    def slot(s, carry):
        @pl.when(used_ref[s] > 0)
        def _():
            wide[:, :bins, :] = echo_ref[s].astype(F32)
            for p in range(pulses):
                slope = params_ref[s, p : p + 1, :]
                shift = params_ref[s, pulses + p : pulses + p + 1, :]
                turn = phase_ref[...] * shift
                rowturn[p, 0] = jnp.cos(turn)
                rowturn[p, 1] = jnp.sin(turn)
                for q in range(4):
                    angle = (512 * sub + 128 * q + lane).astype(F32) * slope
                    ramp[p, 0, q] = jnp.cos(angle)
                    ramp[p, 1, q] = jnp.sin(angle)

            def gather(pair, c):
                for plane in range(2 * pulses):
                    halves = []
                    for h in range(2):
                        begin = start_ref[2 * pair + h]
                        tile = begin // 128
                        off = begin - 128 * tile
                        spot = 2 * plane + h
                        turned[spot] = pltpu.roll(
                            wide[plane, pl.ds(tile, 32), :], lax.rem(128 - off, 128), 1
                        )
                        ys = [turned[spot, pl.ds(o, 8, stride=3), :] for o in range(5)]
                        first = lane < 128 - off
                        halves.append(
                            [jnp.where(first, ys[j], ys[j + 1]) for j in range(4)]
                        )
                    for j in range(4):
                        both = jnp.concatenate([halves[0][j], halves[1][j]], axis=0)
                        lhs[plane, pl.ds(pl.multiple_of(16 * pair, 16), 16), 128 * j : 128 * j + 128] = both.astype(BF16)
                return c

            lax.fori_loop(0, rows // 2, gather, 0)
            for plane in range(2 * pulses):
                product[plane, :, 0:256] = jnp.dot(
                    lhs[plane, :, 0:256], table_ref[0:256, 0:256], preferred_element_type=F32
                )
                product[plane, :, 256:512] = jnp.dot(
                    lhs[plane], table_ref[:, 256:512], preferred_element_type=F32
                )

            def turn_row(r, c):
                at = pl.ds(pl.multiple_of(8 * r, 8), 8)
                for q in range(4):
                    total_re = acc[0, r, q]
                    total_im = acc[1, r, q]
                    for p in range(pulses):
                        row_re = rowturn[p, 0, pl.ds(r, 1), :]
                        row_im = rowturn[p, 1, pl.ds(r, 1), :]
                        ramp_re = ramp[p, 0, q]
                        ramp_im = ramp[p, 1, q]
                        re = ramp_re * row_re - ramp_im * row_im
                        im = ramp_re * row_im + ramp_im * row_re
                        value_re = product[2 * p, at, 128 * q : 128 * q + 128]
                        value_im = product[2 * p + 1, at, 128 * q : 128 * q + 128]
                        total_re = total_re + (value_re * re - value_im * im)
                        total_im = total_im + (value_re * im + value_im * re)
                    acc[0, r, q] = total_re
                    acc[1, r, q] = total_im
                return c

            lax.fori_loop(0, rows, turn_row, 0)

        return carry

    lax.fori_loop(0, n, slot, 0)

    def place(r, c):
        for plane in range(2):
            for q in range(4):
                image[pl.ds((plane * rows + r) * KBLOCKS + q, QUADS, stride=4), :] = (
                    acc[plane, r, q] * scale
                )
        return c

    lax.fori_loop(0, rows, place, 0)

    together = 16 // share
    main = 2 * rows * share

    def emit(i, c):
        for g in range(groups):
            parts = [
                image[pl.ds((i * together + h) * KBLOCKS + share * g, share), :]
                for h in range(together)
            ]
            out_ref[g, pl.ds(pl.multiple_of(16 * i, 16), 16), :] = jnp.concatenate(
                parts, axis=0
            ).astype(BF16)
        return c

    lax.fori_loop(0, 2 * rows // together, emit, 0)
    wide_lane = lax.broadcasted_iota(jnp.int32, (rows, 128), 1)
    for g in range(groups):
        after = min(share * (g + 1), KBLOCKS - 1)
        before = max(share * g - 1, 0)
        for plane in range(2):
            edge = jnp.where(
                wide_lane < 64,
                image[pl.ds(plane * rows * KBLOCKS + after, rows, stride=KBLOCKS), :],
                image[pl.ds(plane * rows * KBLOCKS + before, rows, stride=KBLOCKS), :],
            )
            out_ref[g, main + plane * rows : main + (plane + 1) * rows, :] = edge.astype(BF16)


def partial_image(used, starts, echo, params, phases, table, pulses, groups):
    n, planes, bins, _ = echo.shape
    rows = phases.shape[0]
    share = KBLOCKS // groups
    vmem = pl.BlockSpec(memory_space=pltpu.VMEM)
    smem = pl.BlockSpec(memory_space=pltpu.SMEM)
    return pl.pallas_call(
        functools.partial(image_kernel, pulses, groups),
        out_shape=jax.ShapeDtypeStruct((groups, 2 * rows * share + 2 * rows, 128), BF16),
        in_specs=[smem, smem, vmem, vmem, vmem, vmem],
        out_specs=vmem,
        scratch_shapes=[
            pltpu.VMEM((planes, bins + 8, 128), F32),
            pltpu.VMEM((2 * planes, 32, 128), F32),
            pltpu.VMEM((planes, rows * QUADS, 512), BF16),
            pltpu.VMEM((planes, rows * QUADS, 512), F32),
            pltpu.VMEM((pulses, 2, 4, 8, 128), F32),
            pltpu.VMEM((pulses, 2, rows, 128), F32),
            pltpu.VMEM((2, rows, 4, 8, 128), F32),
            pltpu.VMEM((2 * rows * KBLOCKS, 128), F32),
        ],
        compiler_params=pltpu.CompilerParams(vmem_limit_bytes=48 * 1024 * 1024),
    )(used, starts, echo, params, phases, table)


def refine_kernel(
    rows,
    groups,
    tiles,
    part_ref,
    out_ref,
    got,
    first,
    second,
    halo,
    sends,
    recvs,
    halo_sends,
    halo_recvs,
):
    share = KBLOCKS // groups
    blocks = share + 1
    group = lax.axis_index("pulse")
    tile = lax.axis_index("tile")
    barrier = pltpu.get_barrier_semaphore()
    for d in range(1, groups):
        pl.semaphore_signal(
            barrier, inc=1, device_id={"pulse": lax.rem(group + d, groups)}, device_id_type=MESH
        )

    @pl.when(tile > 0)
    def _():
        pl.semaphore_signal(barrier, inc=1, device_id={"tile": tile - 1}, device_id_type=MESH)

    @pl.when(tile < tiles - 1)
    def _():
        pl.semaphore_signal(barrier, inc=1, device_id={"tile": tile + 1}, device_id_type=MESH)

    around = (tile > 0).astype(jnp.int32) + (tile < tiles - 1).astype(jnp.int32)
    pl.semaphore_wait(barrier, groups - 1 + around)

    copies = []
    for d in range(1, groups):
        target = lax.rem(group + d, groups)
        copy = pltpu.make_async_remote_copy(
            src_ref=part_ref.at[target],
            dst_ref=got.at[d - 1],
            send_sem=sends.at[d - 1],
            recv_sem=recvs.at[d - 1],
            device_id={"pulse": target},
            device_id_type=MESH,
        )
        copy.start()
        copies.append(copy)
    for copy in copies:
        copy.wait()

    main = 2 * rows * share
    total = part_ref[group].astype(F32)
    for d in range(1, groups):
        total = total + got[d - 1].astype(F32)
    for plane in range(2):
        first[plane, HALO : HALO + rows, 0:share, :] = total[
            plane * rows * share : (plane + 1) * rows * share
        ].reshape(rows, share, 128)
        for r in range(rows):
            at = main + plane * rows + r
            first[plane, HALO + r, share:blocks, :] = total[at : at + 1]

    def upward():
        return pltpu.make_async_remote_copy(
            src_ref=first.at[:, pl.ds(HALO, HALO)],
            dst_ref=halo.at[1],
            send_sem=halo_sends.at[1],
            recv_sem=halo_recvs.at[1],
            device_id={"tile": tile - 1},
            device_id_type=MESH,
        )

    def downward():
        return pltpu.make_async_remote_copy(
            src_ref=first.at[:, pl.ds(rows, HALO)],
            dst_ref=halo.at[0],
            send_sem=halo_sends.at[0],
            recv_sem=halo_recvs.at[0],
            device_id={"tile": tile + 1},
            device_id_type=MESH,
        )

    @pl.when(tile > 0)
    def _():
        upward().start()

    @pl.when(tile < tiles - 1)
    def _():
        downward().start()

    @pl.when(tile > 0)
    def _():
        downward().wait_recv()
        first[:, 0:HALO] = halo[0]

    @pl.when(tile == 0)
    def _():
        first[:, 0:HALO] = jnp.zeros_like(first[:, 0:HALO])

    @pl.when(tile < tiles - 1)
    def _():
        upward().wait_recv()
        first[:, HALO + rows :] = halo[1]

    @pl.when(tile == tiles - 1)
    def _():
        first[:, HALO + rows :] = jnp.zeros_like(first[:, 0:HALO])

    @pl.when(tile > 0)
    def _():
        upward().wait_send()

    @pl.when(tile < tiles - 1)
    def _():
        downward().wait_send()

    shape = (2, blocks, 128)
    lane = lax.broadcasted_iota(jnp.int32, shape, 2)
    block = lax.broadcasted_iota(jnp.int32, shape, 1)
    column = group * share * 128 + block * 128 + lane
    edge_column = jnp.where(lane < 64, column, group * share * 128 + lane - 128)
    column = jnp.where(block == share, edge_column, column)
    column_in = (column >= 0) & (column < NCOL)
    has_right = (column >= 0) & (column < NCOL - 1)
    keep_row = jnp.where(column_in, 1.0, 0.0).astype(F32)
    keep_col = jnp.where(has_right, 1.0, 0.0).astype(F32)
    row_base = tile * rows - HALO
    grid_rows = tiles * rows

    def right_of(x):
        following = jnp.concatenate([x[:, 1:], x[:, :1]], axis=1)
        return jnp.where(lane == 127, pltpu.roll(following, 127, 2), pltpu.roll(x, 127, 2))

    def left_of(x):
        preceding = jnp.concatenate([x[:, share:], x[:, :share]], axis=1)
        return jnp.where(lane == 0, pltpu.roll(preceding, 1, 2), pltpu.roll(x, 1, 2))

    def flux(source, i):
        here = source[:, i, 0:blocks, :]
        row = row_base + i
        row_in = ((row >= 0) & (row < grid_rows)).astype(F32)
        below_in = ((row >= 0) & (row < grid_rows - 1)).astype(F32)
        down = (source[:, i + 1, 0:blocks, :] - here) * (keep_row * below_in)
        right = (right_of(here) - here) * (keep_col * row_in)
        square = jnp.sum(down * down + right * right, axis=0, keepdims=True) + floor_square
        inverse = lax.rsqrt(square)
        return here, down * inverse, right * inverse

    def sweep(source, low, high, write):
        _, above, _ = flux(source, low - 1)

        def one(i, above):
            here, down, right = flux(source, i)
            divergence = down - above + right - left_of(right)
            base = first[:, i, 0:blocks, :]
            write(i, here - step_size * (here - base - tv_weight * divergence))
            return down

        lax.fori_loop(low, high, one, above, unroll=2)

    def write_second(i, value):
        second[:, i, 0:blocks, :] = value

    def write_out(i, value):
        out_ref[:, i - HALO] = value[:, 0:share]

    sweep(first, 1, rows + 2 * HALO - 1, write_second)
    sweep(second, 2, rows + 2 * HALO - 2, write_out)


def refine(partial, rows, groups, tiles):
    share = KBLOCKS // groups
    padded = -(-(share + 1) // 8) * 8
    extent = rows + 2 * HALO
    return pl.pallas_call(
        functools.partial(refine_kernel, rows, groups, tiles),
        out_shape=jax.ShapeDtypeStruct((2, rows, share, 128), F32),
        in_specs=[pl.BlockSpec(memory_space=pltpu.VMEM)],
        out_specs=pl.BlockSpec(memory_space=pltpu.VMEM),
        scratch_shapes=[
            pltpu.VMEM((groups - 1,) + partial.shape[1:], BF16),
            pltpu.VMEM((2, extent, padded, 128), F32),
            pltpu.VMEM((2, extent, padded, 128), F32),
            pltpu.VMEM((2, 2, HALO, padded, 128), F32),
            pltpu.SemaphoreType.DMA((groups - 1,)),
            pltpu.SemaphoreType.DMA((groups - 1,)),
            pltpu.SemaphoreType.DMA((2,)),
            pltpu.SemaphoreType.DMA((2,)),
        ],
        compiler_params=pltpu.CompilerParams(
            collective_id=1, has_side_effects=True, vmem_limit_bytes=48 * 1024 * 1024
        ),
    )(partial)


def body(echoes, pulse_slope, pulse_shift, footprint, band_start, row_phase):
    tiles = lax.axis_size("tile")
    groups = lax.axis_size("pulse")
    tile = lax.axis_index("tile")
    held, pulses = pulse_slope.shape
    rows = band_start.shape[0]
    bins = echoes.shape[3] // 128
    lists = footprint[0]
    wanted = [jnp.any(lists == tile * held + b, axis=1) for b in range(held)]
    planes = echoes.reshape(held, pulses * 2, bins, 128)
    params = jnp.concatenate([pulse_slope, pulse_shift], axis=1).astype(F32)
    params = jnp.pad(params, ((0, 0), (0, -(2 * pulses) % 8)))
    blocks = jnp.broadcast_to(planes[0][None], (tiles,) + planes.shape[1:])
    values = jnp.broadcast_to(params[0][None], (tiles, params.shape[1]))
    for b in range(1, held):
        blocks = jnp.where(wanted[b][:, None, None, None], planes[b][None], blocks)
        values = jnp.where(wanted[b][:, None], params[b][None], values)
    values = jnp.broadcast_to(values[:, :, None], values.shape + (128,))
    got, got_params = exchange(blocks, values)

    own_list = lax.dynamic_index_in_dim(lists, tile, axis=0, keepdims=False)
    sources = jnp.arange(tiles, dtype=jnp.int32)
    used = jnp.any(
        (own_list[None, :] >= 0) & (own_list[None, :] // held == sources[:, None]), axis=1
    ).astype(jnp.int32)
    phases = jnp.broadcast_to(row_phase[:, None], (rows, 128))
    table = jnp.asarray(interpolation_table(), BF16)
    partial = partial_image(used, band_start, got, got_params, phases, table, pulses, groups)
    refined = refine(partial, rows, groups, tiles)
    return refined.reshape(2, rows, NCOL // groups)


def solution(mesh):
    in_specs = (
        P(("pulse", "tile"), None, None, None),
        P(("pulse", "tile"), None),
        P(("pulse", "tile"), None),
        P("pulse", None, None),
        P("tile"),
        P("tile"),
    )
    out_specs = P(None, "tile", "pulse")
    return jax.shard_map(body, mesh=mesh, in_specs=in_specs, out_specs=out_specs, check_vma=False)
```

time: 391 us -> 86 us (0.22)
  the two profiles are of different devices: /device:TPU:0 before, /device:TPU:25 now
where the time goes in v1:
time: 86 us; the launch traced here: 85.7 us
  Pallas kernels  77.3 us (90%)
  local copies, waits for them, and re-layouts  6.81 us (8%)
  other arithmetic  1.53 us (2%)
    pallas_call x1, Pallas kernels, refine(): pl.pallas_call(functools.partial(refine_kernel, rows, groups, tiles), out...  36.8 us
    pallas_call x1, Pallas kernels, exchange(): pl.pallas_call(functools.partial(exchange_kernel, n), out_shape=(jax.Shap...  24.4 us
    pallas_call x1, Pallas kernels, partial_image(): pl.pallas_call(functools.partial(image_kernel, pulses, groups), out_shape...  16 us
    unnamed x16, local copies, waits for them, and re-layouts  3.92 us

profile of v1, /device:TPU:25, one launch (start us, length us, event | category | flops | bytes accessed | tf_op | source)
XLA Modules:
  0.0 85.7 jit_solution(9242141201122159618)
XLA Ops:
  0.0 0.7 copy-done.4
  0.7 0.1 fusion.1
  0.8 0.1 compare_reduce_fusion
  1.0 1.2 %fusion.6 = (bf16[1,2,2,16384]{3,2,1,0:T(2,128)(2,1)S(1)}, bf16[1,2,2,16384]{3,2,1,0:T(2,128)(2,1)S(1)}) fusion(bf16[2,2,2,16384]{3,2,1,0:T(2,128)(2,1)} %param.7), kind=kLoop, calls=%fused_computation.20 | loop fusion | bytes 524288 | tf_op jit(solution)/shard_map/slice | solution.py:470
  2.1 0.1 broadcast_in_dim.68
  2.2 0.1 broadcast_in_dim.70
  2.3 0.0 copy-start.6
  2.4 0.0 copy-start.7
  2.4 1.1 %broadcast_select_fusion.blocks_ref = bf16[8,4,128,128]{3,2,1,0:T(8,128)(2,1)} fusion(pred[8]{0:T(512)(128)(4,1)S(1)} %compare_reduce_fusion, bf16[4,128,128]{2,1,0:T(8,128)(2,1)S(1)} %broadcast_in_dim.70, bf16[4,128,128]{2,1,0:T(8,128)(2,1)S(1)} %broadcast_in_dim.68), kind=kLoop, calls=%fused_computation | loop fusion | flops 524288 | bytes 1310728 | tf_op jit(solution)/shard_map/jit(_where)/select_n | solution.py:470
  3.5 0.0 copy-done.6
  3.5 0.0 copy-done.7
  3.5 0.1 fusion.5
  3.6 0.1 broadcast_select_fusion.1
  3.7 0.7 broadcast_in_dim.77.params_ref
  4.3 24.4 %shard_map.73 = (bf16[8,4,128,128]{3,2,1,0:T(8,128)(2,1)}, f32[8,8,128]{2,1,0:T(8,128)}) custom-call(bf16[8,4,128,128]{3,2,1,0:T(8,128)(2,1)} %broadcast_select_fusion.blocks_ref, f32[8,8,128]{2,1,0:T(8,128)} %broadcast_in_dim.77.params_ref), custom_call_target="tpu_custom_call" | custom-call | tf_op jit(solution)/shard_map/pallas_call | solution.py:78
  28.8 0.0 copy-start.5
  28.8 0.6 copy-done.5
  29.4 0.1 broadcast_in_dim.78.phase_ref
  29.5 0.6 copy-done.3
  30.1 1.2 %copy-done = bf16[8,4,128,128]{3,2,1,0:T(8,128)(2,1)S(1)} copy-done((bf16[8,4,128,128]{3,2,1,0:T(8,128)(2,1)S(1)}, bf16[8,4,128,128]{3,2,1,0:T(8,128)(2,1)}, u32[]{:S(2)}) %copy-start) | copy-done | bytes 1048600
  31.3 0.8 copy-done.2
  32.0 16.0 %shard_map.74.part_ref = bf16[4,576,128]{2,1,0:T(8,128)(2,1)S(1)} custom-call(s32[8]{0:T(128)S(1)} %convert_element_type.6.used_ref, s32[32]{0:T(128)S(1)} %copy-done.3, bf16[8,4,128,128]{3,2,1,0:T(8,128)(2,1)S(1)} %copy-done, f32[8,8,128]{2,1,0:T(8,128)S(1)} %copy-done.2, f32[32,128]{1,0:T(8,128)S(1)} %broadcast_in_dim.78.phase_ref, ...), custom_call_target="tpu_custom_call" | custom-call | tf_op jit(solution)/shard_map/pallas_call | solution.py:239
  48.1 36.8 %shard_map.75 = f32[2,32,8,128]{3,2,1,0:T(8,128)S(1)} custom-call(bf16[4,576,128]{2,1,0:T(8,128)(2,1)S(1)} %shard_map.74.part_ref), custom_call_target="tpu_custom_call" | custom-call | tf_op jit(solution)/shard_map/pallas_call | solution.py:434
  84.9 0.7 reshape.121
  (10 shorter events, 0.0 us)
Async XLA Ops:
  0.0 0.7 copy-start.4
  2.3 1.1 %copy-start.6 = (bf16[2,2]{1,0:T(2,128)(2,1)S(1)}, bf16[2,2]{1,0:T(2,128)(2,1)}, u32[]{:S(2)}) copy-start(bf16[2,2]{1,0:T(2,128)(2,1)} %param.9) | copy-start | bytes 28
  2.4 1.1 %copy-start.7 = (bf16[2,2]{1,0:T(2,128)(2,1)S(1)}, bf16[2,2]{1,0:T(2,128)(2,1)}, u32[]{:S(2)}) copy-start(bf16[2,2]{1,0:T(2,128)(2,1)} %param.8) | copy-start | bytes 28
  4.3 25.1 %copy-start.1 = (bf16[512,512]{1,0:T(8,128)(2,1)S(1)}, bf16[512,512]{1,0:T(8,128)(2,1)}, u32[]{:S(2)}) copy-start(bf16[512,512]{1,0:T(8,128)(2,1)} %constant.35.clone.table_ref) | copy-start | bytes 1572868
  28.8 0.7 copy-start.5
  29.4 0.7 copy-start.3
  30.1 1.2 %copy-start = (bf16[8,4,128,128]{3,2,1,0:T(8,128)(2,1)S(1)}, bf16[8,4,128,128]{3,2,1,0:T(8,128)(2,1)}, u32[]{:S(2)}) copy-start(bf16[8,4,128,128]{3,2,1,0:T(8,128)(2,1)} %get-tuple-element.7.echo_ref) | copy-start | bytes 3145732
  31.3 0.8 copy-start.2

commit v2 on v1

v2 whole, which is shorter than its diff:
```python
import functools

import jax
import jax.numpy as jnp
import numpy as np
from jax import lax
from jax.experimental import pallas as pl
from jax.experimental.pallas import tpu as pltpu
from jax.sharding import PartitionSpec as P

NCOL = 4096
ITERS = 2
KBLOCKS = NCOL // 128
QUADS = KBLOCKS // 4
HALO = ITERS

step_size = 0.5
tv_weight = 0.4
floor_square = 0.25

MESH = pl.DeviceIdType.MESH
F32 = jnp.float32
BF16 = jnp.bfloat16


def interpolation_table():
    columns = np.arange(128)
    position = 3 * columns + 4
    base = position // 4
    f = (position % 4) / 4.0
    weights = [
        (-(f**3) + 2 * f**2 - f) / 2,
        (3 * f**3 - 5 * f**2 + 2) / 2,
        (-3 * f**3 + 4 * f**2 + f) / 2,
        (f**3 - f**2) / 2,
    ]
    table = np.zeros((512, 512), np.float32)
    for q in range(4):
        for shift, weight in zip(range(-1, 3), weights):
            table[96 * q + base + shift, 128 * q + columns] += weight
    return table


def sine_cosine(angle):
    turns = jnp.floor(angle * 0.6366197723675814 + 0.5)
    rest = angle - turns * 1.5703125
    rest = rest - turns * 4.837512969970703125e-4
    rest = rest - turns * 7.549789948768648e-8
    square = rest * rest
    sine = rest + rest * square * (
        -1.6666654611e-1 + square * (8.3321608736e-3 - square * 1.9515295891e-4)
    )
    cosine = (1.0 - 0.5 * square) + square * square * (
        4.166664568298827e-2 + square * (-1.388731625493765e-3 + square * 2.443315711809948e-5)
    )
    quarter = turns - 4.0 * jnp.floor(turns * 0.25)
    odd = (quarter == 1.0) | (quarter == 3.0)
    sine_sign = jnp.where(quarter >= 2.0, -1.0, 1.0)
    cosine_sign = jnp.where((quarter == 1.0) | (quarter == 2.0), -1.0, 1.0)
    return (
        sine_sign * jnp.where(odd, cosine, sine),
        cosine_sign * jnp.where(odd, sine, cosine),
    )


def kernel(
    held,
    pulses,
    rows,
    groups,
    n,
    lists_ref,
    start_ref,
    echo_ref,
    phase_ref,
    table_ref,
    out_ref,
    picked,
    got,
    wide,
    turned,
    lhs,
    product,
    ramp,
    rowturn,
    acc,
    image,
    part,
    got_part,
    first,
    second,
    halo,
    sends,
    recvs,
    part_sends,
    part_recvs,
    halo_sends,
    halo_recvs,
):
    bins = (echo_ref.shape[1] - 16) // (2 * pulses)
    planes = 2 * pulses
    share = KBLOCKS // groups
    blocks = share + 1
    scale = float(pulses * n * groups) ** -0.5
    group = lax.axis_index("pulse")
    tile = lax.axis_index("tile")
    power = n & (n - 1) == 0

    def partner(d):
        if not power:
            return lax.rem(n + d - tile, n)
        other = tile
        bit = 1
        while bit < n:
            other = other + ((d // bit) % 2) * bit * (1 - 2 * ((tile // bit) % 2))
            bit *= 2
        return other

    barrier = pltpu.get_barrier_semaphore()
    for d in range(1, groups):
        pl.semaphore_signal(
            barrier, inc=1, device_id={"pulse": lax.rem(group + d, groups)}, device_id_type=MESH
        )
    for d in range(1, n):
        pl.semaphore_signal(
            barrier, inc=1, device_id={"tile": lax.rem(tile + d, n)}, device_id_type=MESH
        )

    def names(strip, number):
        found = lists_ref[strip, 0] == number
        for j in range(1, lists_ref.shape[1]):
            found = found | (lists_ref[strip, j] == number)
        return found

    def pick(d, c):
        other = partner(d)
        block = echo_ref[0]
        for b in range(1, held):
            block = jnp.where(names(other, tile * held + b), echo_ref[b], block)
        picked[d] = block
        return c

    lax.fori_loop(0, n, pick, 0)
    pl.semaphore_wait(barrier, n - 1 + groups - 1)

    def block_copy(d):
        return pltpu.make_async_remote_copy(
            src_ref=picked.at[d],
            dst_ref=got.at[d],
            send_sem=sends.at[d],
            recv_sem=recvs.at[d],
            device_id={"tile": partner(d)},
            device_id_type=MESH,
        )

    def send(i, c):
        block_copy(n - i).start()
        return c

    lax.fori_loop(1, n, send, 0)

    lane = lax.broadcasted_iota(jnp.int32, (8, 128), 1)
    sub = lax.broadcasted_iota(jnp.int32, (8, 128), 0)
    wide[:, bins:, :] = jnp.zeros((planes, wide.shape[1] - bins, 128), F32)
    acc[...] = jnp.zeros_like(acc)
    column_in_quad = (512 * sub + lane).astype(F32)

    def compute(d, block):
        source = partner(d)
        used = names(tile, source * held)
        for b in range(1, held):
            used = used | names(tile, source * held + b)
        weight = jnp.where(used, 1.0, 0.0).astype(F32)
        wide[:, :bins, :] = block[: planes * bins].astype(F32).reshape(planes, bins, 128)
        tail = block[planes * bins :].astype(F32)
        for p in range(pulses):
            slope = tail[p : p + 1]
            shift = tail[pulses + p : pulses + p + 1]
            turn_im, turn_re = sine_cosine(phase_ref[...] * shift)
            rowturn[p, 0] = turn_re
            rowturn[p, 1] = turn_im
            im, re = sine_cosine(column_in_quad * slope)
            step_im, step_re = sine_cosine(jnp.broadcast_to(128.0 * slope, (8, 128)))
            re = re * weight
            im = im * weight
            for q in range(4):
                ramp[p, 0, q] = re
                ramp[p, 1, q] = im
                re, im = re * step_re - im * step_im, re * step_im + im * step_re

        def gather(pair, c):
            for plane in range(planes):
                halves = []
                for h in range(2):
                    begin = start_ref[2 * pair + h]
                    at = begin // 128
                    off = begin - 128 * at
                    spot = 2 * plane + h
                    turned[spot] = pltpu.roll(
                        wide[plane, pl.ds(at, 32), :], lax.rem(128 - off, 128), 1
                    )
                    ys = [turned[spot, pl.ds(o, 8, stride=3), :] for o in range(5)]
                    keep = lane < 128 - off
                    halves.append([jnp.where(keep, ys[j], ys[j + 1]) for j in range(4)])
                for j in range(4):
                    both = jnp.concatenate([halves[0][j], halves[1][j]], axis=0)
                    lhs[
                        plane, pl.ds(pl.multiple_of(16 * pair, 16), 16), 128 * j : 128 * j + 128
                    ] = both.astype(BF16)
            return c

        lax.fori_loop(0, rows // 2, gather, 0, unroll=2)
        for plane in range(planes):
            product[plane, :, 0:256] = jnp.dot(
                lhs[plane, :, 0:256], table_ref[0:256, 0:256], preferred_element_type=F32
            )
            product[plane, :, 256:512] = jnp.dot(
                lhs[plane], table_ref[:, 256:512], preferred_element_type=F32
            )

        def turn_row(r, c):
            at = pl.ds(pl.multiple_of(8 * r, 8), 8)
            for q in range(4):
                total_re = acc[0, r, q]
                total_im = acc[1, r, q]
                for p in range(pulses):
                    row_re = rowturn[p, 0, pl.ds(r, 1), :]
                    row_im = rowturn[p, 1, pl.ds(r, 1), :]
                    ramp_re = ramp[p, 0, q]
                    ramp_im = ramp[p, 1, q]
                    re = ramp_re * row_re - ramp_im * row_im
                    im = ramp_re * row_im + ramp_im * row_re
                    value_re = product[2 * p, at, 128 * q : 128 * q + 128]
                    value_im = product[2 * p + 1, at, 128 * q : 128 * q + 128]
                    total_re = total_re + (value_re * re - value_im * im)
                    total_im = total_im + (value_re * im + value_im * re)
                acc[0, r, q] = total_re
                acc[1, r, q] = total_im
            return c

        lax.fori_loop(0, rows, turn_row, 0, unroll=2)

    def slot(d, c):
        block_copy(d).wait_recv()
        compute(d, got[d])
        return c

    compute(0, picked[0])
    lax.fori_loop(1, n, slot, 0)

    def sent(d, c):
        block_copy(d).wait_send()
        return c

    lax.fori_loop(1, n, sent, 0)

    def place(r, c):
        for plane in range(2):
            for q in range(4):
                image[pl.ds((plane * rows + r) * KBLOCKS + q, QUADS, stride=4), :] = (
                    acc[plane, r, q] * scale
                )
        return c

    lax.fori_loop(0, rows, place, 0, unroll=2)

    together = 16 // share
    main = 2 * rows * share
    wide_lane = lax.broadcasted_iota(jnp.int32, (rows, 128), 1)

    def emit_for(g):
        def emit(i, c):
            parts = [
                image[pl.ds((i * together + h) * KBLOCKS + share * g, share), :]
                for h in range(together)
            ]
            part[g, pl.ds(pl.multiple_of(16 * i, 16), 16), :] = jnp.concatenate(
                parts, axis=0
            ).astype(BF16)
            return c

        lax.fori_loop(0, 2 * rows // together, emit, 0, unroll=4)
        after = jnp.minimum(share * (g + 1), KBLOCKS - 1)
        before = jnp.maximum(share * g - 1, 0)
        for plane in range(2):
            edge = jnp.where(
                wide_lane < 64,
                image[pl.ds(plane * rows * KBLOCKS + after, rows, stride=KBLOCKS), :],
                image[pl.ds(plane * rows * KBLOCKS + before, rows, stride=KBLOCKS), :],
            )
            part[g, main + plane * rows : main + (plane + 1) * rows, :] = edge.astype(BF16)

    copies = []
    for d in range(groups - 1, 0, -1):
        target = lax.rem(group + d, groups)
        emit_for(target)
        copy = pltpu.make_async_remote_copy(
            src_ref=part.at[target],
            dst_ref=got_part.at[d - 1],
            send_sem=part_sends.at[d - 1],
            recv_sem=part_recvs.at[d - 1],
            device_id={"pulse": target},
            device_id_type=MESH,
        )
        copy.start()
        copies.append(copy)
    emit_for(group)
    for copy in copies:
        copy.wait()

    total = part[group].astype(F32)
    for d in range(1, groups):
        total = total + got_part[d - 1].astype(F32)
    for plane in range(2):
        first[plane, HALO : HALO + rows, 0:share, :] = total[
            plane * rows * share : (plane + 1) * rows * share
        ].reshape(rows, share, 128)
        for r in range(rows):
            at = main + plane * rows + r
            first[plane, HALO + r, share:blocks, :] = total[at : at + 1]

    def upward():
        return pltpu.make_async_remote_copy(
            src_ref=first.at[:, pl.ds(HALO, HALO)],
            dst_ref=halo.at[1],
            send_sem=halo_sends.at[1],
            recv_sem=halo_recvs.at[1],
            device_id={"tile": tile - 1},
            device_id_type=MESH,
        )

    def downward():
        return pltpu.make_async_remote_copy(
            src_ref=first.at[:, pl.ds(rows, HALO)],
            dst_ref=halo.at[0],
            send_sem=halo_sends.at[0],
            recv_sem=halo_recvs.at[0],
            device_id={"tile": tile + 1},
            device_id_type=MESH,
        )

    @pl.when(tile > 0)
    def _():
        upward().start()

    @pl.when(tile < n - 1)
    def _():
        downward().start()

    @pl.when(tile > 0)
    def _():
        downward().wait_recv()
        first[:, 0:HALO] = halo[0]

    @pl.when(tile == 0)
    def _():
        first[:, 0:HALO] = jnp.zeros_like(first[:, 0:HALO])

    @pl.when(tile < n - 1)
    def _():
        upward().wait_recv()
        first[:, HALO + rows :] = halo[1]

    @pl.when(tile == n - 1)
    def _():
        first[:, HALO + rows :] = jnp.zeros_like(first[:, 0:HALO])

    @pl.when(tile > 0)
    def _():
        upward().wait_send()

    @pl.when(tile < n - 1)
    def _():
        downward().wait_send()


    row_base = tile * rows - HALO
    grid_rows = n * rows

    def sweep(source, low, high, write):
        def chunk(begin, count):
            shape = (2, count + 1, blocks, 128)
            lane = lax.broadcasted_iota(jnp.int32, shape, 3)
            block = lax.broadcasted_iota(jnp.int32, shape, 2)
            row = row_base + begin - 1 + lax.broadcasted_iota(jnp.int32, shape, 1)
            wrap = jnp.where((block == share) & (lane >= 64), 128 * blocks, 0)
            column = group * share * 128 + block * 128 + lane - wrap
            inside = (column >= 0) & (column < NCOL) & (row >= 0) & (row < grid_rows)
            keep_down = jnp.where(inside & (row < grid_rows - 1), 1.0, 0.0)
            keep_right = jnp.where(inside & (column < NCOL - 1), 1.0, 0.0)
            held = source[:, begin - 1 : begin + count + 1, 0:blocks, :]
            here = held[:, :-1]
            following = jnp.concatenate([here[:, :, 1:], here[:, :, :1]], axis=2)
            right = jnp.where(lane == 127, pltpu.roll(following, 127, 3), pltpu.roll(here, 127, 3))
            down = (held[:, 1:] - here) * keep_down
            right = (right - here) * keep_right
            square = jnp.sum(down * down + right * right, axis=0, keepdims=True) + floor_square
            inverse = lax.rsqrt(square)
            down = down * inverse
            right = right * inverse
            preceding = jnp.concatenate([right[:, :, share:], right[:, :, :share]], axis=2)
            left = jnp.where(lane == 0, pltpu.roll(preceding, 1, 3), pltpu.roll(right, 1, 3))
            divergence = (down[:, 1:] - down[:, :-1]) + (right - left)[:, 1:]
            here = here[:, 1:]
            base = first[:, begin : begin + count, 0:blocks, :]
            write(begin, count, here - step_size * (here - base - tv_weight * divergence))

        for begin in range(low, high, 4):
            chunk(begin, min(4, high - begin))

    def write_second(begin, count, value):
        second[:, begin : begin + count, 0:blocks, :] = value

    def write_out(begin, count, value):
        out_ref[:, begin - HALO : begin - HALO + count] = value[:, :, 0:share]

    sweep(first, 1, rows + 2 * HALO - 1, write_second)
    sweep(second, HALO, rows + HALO, write_out)


def body(echoes, pulse_slope, pulse_shift, footprint, band_start, row_phase):
    n = lax.axis_size("tile")
    groups = lax.axis_size("pulse")
    held, pulses = pulse_slope.shape
    rows = band_start.shape[0]
    bins = echoes.shape[3] // 128
    planes = 2 * pulses
    share = KBLOCKS // groups
    values = jnp.concatenate([pulse_slope, pulse_shift], axis=1)
    values = jnp.pad(values, ((0, 0), (0, 16 - 2 * pulses)))
    values = jnp.broadcast_to(values[:, :, None], (held, 16, 128))
    message = jnp.concatenate([echoes.reshape(held, planes * bins, 128), values], axis=1)
    phases = jnp.broadcast_to(row_phase[:, None], (rows, 128))
    table = jnp.asarray(interpolation_table(), BF16)

    vmem = pl.BlockSpec(memory_space=pltpu.VMEM)
    smem = pl.BlockSpec(memory_space=pltpu.SMEM)
    padded = -(-(share + 1) // 8) * 8
    extent = rows + 2 * HALO
    slot = (planes * bins + 16, 128)
    piece = (2 * rows * share + 2 * rows, 128)
    dma = pltpu.SemaphoreType.DMA
    refined = pl.pallas_call(
        functools.partial(kernel, held, pulses, rows, groups, n),
        out_shape=jax.ShapeDtypeStruct((2, rows, share, 128), F32),
        in_specs=[smem, smem, vmem, vmem, vmem],
        out_specs=vmem,
        scratch_shapes=[
            pltpu.VMEM((n,) + slot, BF16),
            pltpu.VMEM((n,) + slot, BF16),
            pltpu.VMEM((planes, bins + 8, 128), F32),
            pltpu.VMEM((2 * planes, 32, 128), F32),
            pltpu.VMEM((planes, rows * QUADS, 512), BF16),
            pltpu.VMEM((planes, rows * QUADS, 512), F32),
            pltpu.VMEM((pulses, 2, 4, 8, 128), F32),
            pltpu.VMEM((pulses, 2, rows, 128), F32),
            pltpu.VMEM((2, rows, 4, 8, 128), F32),
            pltpu.VMEM((2 * rows * KBLOCKS, 128), F32),
            pltpu.VMEM((groups,) + piece, BF16),
            pltpu.VMEM((groups - 1,) + piece, BF16),
            pltpu.VMEM((2, extent, padded, 128), F32),
            pltpu.VMEM((2, extent, padded, 128), F32),
            pltpu.VMEM((2, 2, HALO, padded, 128), F32),
            dma((n,)),
            dma((n,)),
            dma((groups - 1,)),
            dma((groups - 1,)),
            dma((2,)),
            dma((2,)),
        ],
        compiler_params=pltpu.CompilerParams(
            collective_id=0, has_side_effects=True, vmem_limit_bytes=48 * 1024 * 1024
        ),
    )(footprint[0], band_start, message, phases, table)
    return refined.reshape(2, rows, NCOL // groups)


def solution(mesh):
    in_specs = (
        P(("pulse", "tile"), None, None, None),
        P(("pulse", "tile"), None),
        P(("pulse", "tile"), None),
        P("pulse", None, None),
        P("tile"),
        P("tile"),
    )
    out_specs = P(None, "tile", "pulse")
    return jax.shard_map(body, mesh=mesh, in_specs=in_specs, out_specs=out_specs, check_vma=False)
```

time: 86 us -> 60.8 us (0.71)
  the two profiles are of different devices: /device:TPU:25 before, /device:TPU:0 now
where the time goes in v2:
time: 60.8 us; the launch traced here: 60.6 us
  Pallas kernels  56.4 us (93%)
  local copies, waits for them, and re-layouts  3.39 us (6%)
  other arithmetic  0.77 us (1%)
    pallas_call x1, Pallas kernels, body(): pl.pallas_call(functools.partial(kernel, held, pulses, rows, groups, n),...  56.4 us
    unnamed x8, local copies, waits for them, and re-layouts  1.29 us

profile of v2, /device:TPU:0, one launch (start us, length us, event | category | flops | bytes accessed | tf_op | source)
XLA Modules:
  0.0 60.6 jit_solution(17550656302076655234)
XLA Ops:
  0.0 0.0 copy-start
  0.0 1.2 %reshape.8 = bf16[2,512,128]{2,1,0:T(8,128)(2,1)S(1)} reshape(bf16[2,2,2,16384]{3,2,1,0:T(2,128)(2,1)} %param.7) | data formatting | bytes 524288 | tf_op jit(solution)/shard_map/reshape | solution.py:432
  1.2 0.8 %fusion.2 = bf16[2,16]{1,0:T(2,128)(2,1)S(1)} fusion(bf16[2,2]{1,0:T(2,128)(2,1)} %param.9, bf16[2,2]{1,0:T(2,128)(2,1)} %param.8), kind=kLoop, calls=%fused_computation.4 | loop fusion | flops 224 | bytes 80 | tf_op jit(solution)/shard_map/concatenate | solution.py:429
  2.0 0.1 broadcast_in_dim.4
  2.0 0.0 copy-start.3
  2.1 0.6 %copy-done.3 = f32[32]{0:T(128)S(1)} copy-done((f32[32]{0:T(128)S(1)}, f32[32]{0:T(128)}, u32[]{:S(2)}) %copy-start.3) | copy-done | bytes 152
  2.7 0.0 copy-start.1
  2.7 0.1 broadcast_in_dim.5.phase_ref
  2.8 0.0 copy-start.2
  2.8 0.0 copy-done
  2.8 0.6 %copy-done.1 = s32[1,8,8]{2,1,0:T(8,128)S(1)} copy-done((s32[1,8,8]{2,1,0:T(8,128)S(1)}, s32[1,8,8]{2,1,0:T(8,128)}, u32[]{:S(2)}) %copy-start.1) | copy-done | bytes 280
  3.4 0.0 copy-done.2
  3.4 56.4 %shard_map.73 = f32[2,32,8,128]{3,2,1,0:T(8,128)S(1)} custom-call(s32[8,8]{1,0:T(8,128)S(1)} %bitcast.3, s32[32]{0:T(128)S(1)} %copy-done.2, bf16[2,528,128]{2,1,0:T(8,128)(2,1)S(1)} %pad_maximum_fusion.echo_ref, f32[32,128]{1,0:T(8,128)S(1)} %broadcast_in_dim.5.phase_ref, bf16[512,512]{1,0:T(8,128)(2,1)S(1)} %copy-done), custom_call_target="tpu_custom_call" | custom-call | tf_op jit(solution)/shard_map/pallas_call | solution.py:443
  59.9 0.7 %reshape.9 = f32[2,32,1024]{2,1,0:T(8,128)} reshape(f32[2,32,8,128]{3,2,1,0:T(8,128)S(1)} %shard_map.73) | data formatting | bytes 524288 | tf_op jit(solution)/shard_map/reshape | solution.py:475
  (1 shorter events, 0.0 us)
Async XLA Ops:
  0.0 2.8 %copy-start = (bf16[512,512]{1,0:T(8,128)(2,1)S(1)}, bf16[512,512]{1,0:T(8,128)(2,1)}, u32[]{:S(2)}) copy-start(bf16[512,512]{1,0:T(8,128)(2,1)} %constant.5.clone.table_ref) | copy-start | bytes 1572868
  2.0 0.7 %copy-start.3 = (f32[32]{0:T(128)S(1)}, f32[32]{0:T(128)}, u32[]{:S(2)}) copy-start(f32[32]{0:T(128)} %param.12) | copy-start | bytes 388
  2.7 0.7 %copy-start.1 = (s32[1,8,8]{2,1,0:T(8,128)S(1)}, s32[1,8,8]{2,1,0:T(8,128)}, u32[]{:S(2)}) copy-start(s32[1,8,8]{2,1,0:T(8,128)} %param.10) | copy-start | bytes 772
  2.8 0.7 %copy-start.2 = (s32[32]{0:T(128)S(1)}, s32[32]{0:T(128)}, u32[]{:S(2)}) copy-start(s32[32]{0:T(128)} %start_ref.1) | copy-start | bytes 388

commit v3 on v2

--- a/solution.py
+++ b/solution.py
@@ -71,14 +71,17 @@
     n,
     lists_ref,
     start_ref,
+    echo_hbm,
+    phase_hbm,
+    table_hbm,
+    out_ref,
     echo_ref,
     phase_ref,
     table_ref,
-    out_ref,
+    fetch_sems,
     picked,
     got,
     wide,
-    turned,
     lhs,
     product,
     ramp,
@@ -97,7 +100,7 @@
     halo_sends,
     halo_recvs,
 ):
-    bins = (echo_ref.shape[1] - 16) // (2 * pulses)
+    bins = (echo_hbm.shape[1] - 16) // (2 * pulses)
     planes = 2 * pulses
     share = KBLOCKS // groups
     blocks = share + 1
@@ -116,7 +119,15 @@
             bit *= 2
         return other
 
+    fetch_echo = pltpu.make_async_copy(echo_hbm, echo_ref, fetch_sems.at[0])
+    fetches = [
+        pltpu.make_async_copy(table_hbm, table_ref, fetch_sems.at[1]),
+        pltpu.make_async_copy(phase_hbm, phase_ref, fetch_sems.at[2]),
+    ]
     barrier = pltpu.get_barrier_semaphore()
+    fetch_echo.start()
+    for copy in fetches:
+        copy.start()
     for d in range(1, groups):
         pl.semaphore_signal(
             barrier, inc=1, device_id={"pulse": lax.rem(group + d, groups)}, device_id_type=MESH
@@ -131,6 +142,8 @@
         for j in range(1, lists_ref.shape[1]):
             found = found | (lists_ref[strip, j] == number)
         return found
+
+    fetch_echo.wait()
 
     def pick(d, c):
         other = partner(d)
@@ -165,14 +178,45 @@
     acc[...] = jnp.zeros_like(acc)
     column_in_quad = (512 * sub + lane).astype(F32)
 
-    def compute(d, block):
+    def widen(block):
+        wide[:, :bins, :] = block[: planes * bins].astype(F32).reshape(planes, bins, 128)
+
+    def gather(pair):
+        for plane in range(planes):
+            halves = []
+            for h in range(2):
+                begin = start_ref[2 * pair + h]
+                at = begin // 128
+                off = begin - 128 * at
+                shift = lax.rem(128 - off, 128)
+                keep = lane < 128 - off
+                ys = [
+                    pltpu.roll(wide[plane, pl.ds(at + o, 8, stride=3), :], shift, 1)
+                    for o in range(5)
+                ]
+                halves.append([jnp.where(keep, ys[j], ys[j + 1]) for j in range(4)])
+            for j in range(4):
+                both = jnp.concatenate([halves[0][j], halves[1][j]], axis=0)
+                lhs[plane, pl.ds(pl.multiple_of(16 * pair, 16), 16), 128 * j : 128 * j + 128] = (
+                    both.astype(BF16)
+                )
+
+    def multiply():
+        for plane in range(planes):
+            product[plane, :, 0:256] = jnp.dot(
+                lhs[plane, :, 0:256], table_ref[0:256, 0:256], preferred_element_type=F32
+            )
+            product[plane, :, 256:512] = jnp.dot(
+                lhs[plane], table_ref[:, 256:512], preferred_element_type=F32
+            )
+
+    def phase(d, tail):
         source = partner(d)
         used = names(tile, source * held)
         for b in range(1, held):
             used = used | names(tile, source * held + b)
         weight = jnp.where(used, 1.0, 0.0).astype(F32)
-        wide[:, :bins, :] = block[: planes * bins].astype(F32).reshape(planes, bins, 128)
-        tail = block[planes * bins :].astype(F32)
+        tail = tail.astype(F32)
         for p in range(pulses):
             slope = tail[p : p + 1]
             shift = tail[pulses + p : pulses + p + 1]
@@ -188,46 +232,21 @@
                 ramp[p, 1, q] = im
                 re, im = re * step_re - im * step_im, re * step_im + im * step_re
 
-        def gather(pair, c):
-            for plane in range(planes):
-                halves = []
-                for h in range(2):
-                    begin = start_ref[2 * pair + h]
-                    at = begin // 128
-                    off = begin - 128 * at
-                    spot = 2 * plane + h
-                    turned[spot] = pltpu.roll(
-                        wide[plane, pl.ds(at, 32), :], lax.rem(128 - off, 128), 1
-                    )
-                    ys = [turned[spot, pl.ds(o, 8, stride=3), :] for o in range(5)]
-                    keep = lane < 128 - off
-                    halves.append([jnp.where(keep, ys[j], ys[j + 1]) for j in range(4)])
-                for j in range(4):
-                    both = jnp.concatenate([halves[0][j], halves[1][j]], axis=0)
-                    lhs[
-                        plane, pl.ds(pl.multiple_of(16 * pair, 16), 16), 128 * j : 128 * j + 128
-                    ] = both.astype(BF16)
-            return c
-
-        lax.fori_loop(0, rows // 2, gather, 0, unroll=2)
-        for plane in range(planes):
-            product[plane, :, 0:256] = jnp.dot(
-                lhs[plane, :, 0:256], table_ref[0:256, 0:256], preferred_element_type=F32
-            )
-            product[plane, :, 256:512] = jnp.dot(
-                lhs[plane], table_ref[:, 256:512], preferred_element_type=F32
-            )
-
-        def turn_row(r, c):
-            at = pl.ds(pl.multiple_of(8 * r, 8), 8)
-            for q in range(4):
+    def turn(pair):
+        rows_at = [2 * pair, 2 * pair + 1]
+        row_turn = [
+            [[rowturn[p, part_of, pl.ds(r, 1), :] for part_of in range(2)] for p in range(pulses)]
+            for r in rows_at
+        ]
+        for q in range(4):
+            ramps = [[ramp[p, part_of, q] for part_of in range(2)] for p in range(pulses)]
+            for h, r in enumerate(rows_at):
+                at = pl.ds(pl.multiple_of(8 * r, 8), 8)
                 total_re = acc[0, r, q]
                 total_im = acc[1, r, q]
                 for p in range(pulses):
-                    row_re = rowturn[p, 0, pl.ds(r, 1), :]
-                    row_im = rowturn[p, 1, pl.ds(r, 1), :]
-                    ramp_re = ramp[p, 0, q]
-                    ramp_im = ramp[p, 1, q]
+                    row_re, row_im = row_turn[h][p]
+                    ramp_re, ramp_im = ramps[p]
                     re = ramp_re * row_re - ramp_im * row_im
                     im = ramp_re * row_im + ramp_im * row_re
                     value_re = product[2 * p, at, 128 * q : 128 * q + 128]
@@ -236,17 +255,38 @@
                     total_im = total_im + (value_re * im + value_im * re)
                 acc[0, r, q] = total_re
                 acc[1, r, q] = total_im
-            return c
-
-        lax.fori_loop(0, rows, turn_row, 0, unroll=2)
+
+    def gather_only(pair, c):
+        gather(pair)
+        return c
+
+    def gather_and_turn(pair, c):
+        gather(pair)
+        turn(pair)
+        return c
+
+    def turn_only(pair, c):
+        turn(pair)
+        return c
+
+    tail_rows = slice(planes * bins, planes * bins + 16)
+    widen(picked[0])
+    lax.fori_loop(0, rows // 2, gather_only, 0, unroll=2)
+    for copy in fetches:
+        copy.wait()
+    multiply()
+    phase(0, picked[0, tail_rows])
 
     def slot(d, c):
         block_copy(d).wait_recv()
-        compute(d, got[d])
-        return c
-
-    compute(0, picked[0])
+        widen(got[d])
+        lax.fori_loop(0, rows // 2, gather_and_turn, 0, unroll=2)
+        multiply()
+        phase(d, got[d, tail_rows])
+        return c
+
     lax.fori_loop(1, n, slot, 0)
+    lax.fori_loop(0, rows // 2, turn_only, 0, unroll=2)
 
     def sent(d, c):
         block_copy(d).wait_send()
@@ -435,6 +475,7 @@
 
     vmem = pl.BlockSpec(memory_space=pltpu.VMEM)
     smem = pl.BlockSpec(memory_space=pltpu.SMEM)
+    anywhere = pl.BlockSpec(memory_space=pl.ANY)
     padded = -(-(share + 1) // 8) * 8
     extent = rows + 2 * HALO
     slot = (planes * bins + 16, 128)
@@ -443,13 +484,16 @@
     refined = pl.pallas_call(
         functools.partial(kernel, held, pulses, rows, groups, n),
         out_shape=jax.ShapeDtypeStruct((2, rows, share, 128), F32),
-        in_specs=[smem, smem, vmem, vmem, vmem],
+        in_specs=[smem, smem, anywhere, anywhere, anywhere],
         out_specs=vmem,
         scratch_shapes=[
+            pltpu.VMEM(message.shape, BF16),
+            pltpu.VMEM(phases.shape, F32),
+            pltpu.VMEM(table.shape, BF16),
+            dma((3,)),
             pltpu.VMEM((n,) + slot, BF16),
             pltpu.VMEM((n,) + slot, BF16),
             pltpu.VMEM((planes, bins + 8, 128), F32),
-            pltpu.VMEM((2 * planes, 32, 128), F32),
             pltpu.VMEM((planes, rows * QUADS, 512), BF16),
             pltpu.VMEM((planes, rows * QUADS, 512), F32),
             pltpu.VMEM((pulses, 2, 4, 8, 128), F32),

time: 60.8 us -> 58.5 us (0.962)
  Pallas kernels: 56.4 us -> 54.1 us
    pallas_call x1, Pallas kernels: 56.4 us -> 54.1 us  [body(): pl.pallas_call(functools.partial(kernel, held, pulses, rows, groups, n),...]
where the time goes in v3:
time: 58.5 us; the launch traced here: 58.3 us
  Pallas kernels  54.1 us (92%)
  local copies, waits for them, and re-layouts  3.39 us (6%)
  other arithmetic  0.77 us (1%)
    pallas_call x1, Pallas kernels, body(): pl.pallas_call(functools.partial(kernel, held, pulses, rows, groups, n),...  54.1 us
    unnamed x8, local copies, waits for them, and re-layouts  1.29 us
    reshape x1, local copies, waits for them, and re-layouts, body(): echoes.reshape(held, planes * bins, 128)  1.21 us

profile of v3, /device:TPU:0, one launch (start us, length us, event | category | flops | bytes accessed | tf_op | source)
XLA Modules:
  0.0 58.3 jit_solution(11531908097789773130)
XLA Ops:
  0.0 0.0 copy-start
  0.0 1.2 %reshape.8 = bf16[2,512,128]{2,1,0:T(8,128)(2,1)S(1)} reshape(bf16[2,2,2,16384]{3,2,1,0:T(2,128)(2,1)} %param.7) | data formatting | bytes 524288 | tf_op jit(solution)/shard_map/reshape | solution.py:472
  1.2 0.8 %fusion.2 = bf16[2,16]{1,0:T(2,128)(2,1)S(1)} fusion(bf16[2,2]{1,0:T(2,128)(2,1)} %param.9, bf16[2,2]{1,0:T(2,128)(2,1)} %param.8), kind=kLoop, calls=%fused_computation.4 | loop fusion | flops 224 | bytes 80 | tf_op jit(solution)/shard_map/concatenate | solution.py:469
  2.0 0.1 broadcast_in_dim.4
  2.0 0.0 copy-start.3
  2.1 0.6 %copy-done.3 = f32[32]{0:T(128)S(1)} copy-done((f32[32]{0:T(128)S(1)}, f32[32]{0:T(128)}, u32[]{:S(2)}) %copy-start.3) | copy-done | bytes 152
  2.7 0.0 copy-start.1
  2.7 0.1 broadcast_in_dim.5.phase_hbm
  2.8 0.0 copy-start.2
  2.8 0.0 copy-done
  2.8 0.6 %copy-done.1 = s32[1,8,8]{2,1,0:T(8,128)S(1)} copy-done((s32[1,8,8]{2,1,0:T(8,128)S(1)}, s32[1,8,8]{2,1,0:T(8,128)}, u32[]{:S(2)}) %copy-start.1) | copy-done | bytes 280
  3.4 0.0 copy-done.2
  3.4 54.1 %shard_map.73 = f32[2,32,8,128]{3,2,1,0:T(8,128)S(1)} custom-call(s32[8,8]{1,0:T(8,128)S(1)} %bitcast.3, s32[32]{0:T(128)S(1)} %copy-done.2, bf16[2,528,128]{2,1,0:T(8,128)(2,1)S(1)} %pad_maximum_fusion.echo_hbm, f32[32,128]{1,0:T(8,128)S(1)} %broadcast_in_dim.5.phase_hbm, bf16[512,512]{1,0:T(8,128)(2,1)S(1)} %copy-done), custom_call_target="tpu_custom_call" | custom-call | tf_op jit(solution)/shard_map/pallas_call | solution.py:484
  57.5 0.7 %reshape.9 = f32[2,32,1024]{2,1,0:T(8,128)} reshape(f32[2,32,8,128]{3,2,1,0:T(8,128)S(1)} %shard_map.73) | data formatting | bytes 524288 | tf_op jit(solution)/shard_map/reshape | solution.py:519
  (1 shorter events, 0.0 us)
Async XLA Ops:
  0.0 2.8 %copy-start = (bf16[512,512]{1,0:T(8,128)(2,1)S(1)}, bf16[512,512]{1,0:T(8,128)(2,1)}, u32[]{:S(2)}) copy-start(bf16[512,512]{1,0:T(8,128)(2,1)} %constant.5.clone.table_hbm) | copy-start | bytes 1572868
  2.0 0.7 %copy-start.3 = (f32[32]{0:T(128)S(1)}, f32[32]{0:T(128)}, u32[]{:S(2)}) copy-start(f32[32]{0:T(128)} %param.12) | copy-start | bytes 388
  2.7 0.7 %copy-start.1 = (s32[1,8,8]{2,1,0:T(8,128)S(1)}, s32[1,8,8]{2,1,0:T(8,128)}, u32[]{:S(2)}) copy-start(s32[1,8,8]{2,1,0:T(8,128)} %param.10) | copy-start | bytes 772
  2.8 0.7 %copy-start.2 = (s32[32]{0:T(128)S(1)}, s32[32]{0:T(128)}, u32[]{:S(2)}) copy-start(s32[32]{0:T(128)} %start_ref.1) | copy-start | bytes 388

commit v4 on v3

--- a/solution.py
+++ b/solution.py
@@ -63,6 +63,9 @@
     )
 
 
+NEAR, FAR = 0, 1
+
+
 def kernel(
     held,
     pulses,
@@ -70,16 +73,15 @@
     groups,
     n,
     lists_ref,
-    start_ref,
+    starts_hbm,
     echo_hbm,
     phase_hbm,
     table_hbm,
     out_ref,
-    echo_ref,
+    starts_far,
+    starts,
     phase_ref,
     table_ref,
-    fetch_sems,
-    picked,
     got,
     wide,
     lhs,
@@ -90,42 +92,53 @@
     image,
     part,
     got_part,
+    far_out,
+    far_in,
     first,
     second,
     halo,
+    fetch_sems,
+    info_sends,
+    info_recvs,
     sends,
     recvs,
     part_sends,
     part_recvs,
+    far_sends,
+    far_recvs,
     halo_sends,
     halo_recvs,
 ):
-    bins = (echo_hbm.shape[1] - 16) // (2 * pulses)
     planes = 2 * pulses
+    bins = (echo_hbm.shape[1] - 16) // planes
     share = KBLOCKS // groups
     blocks = share + 1
     scale = float(pulses * n * groups) ** -0.5
     group = lax.axis_index("pulse")
     tile = lax.axis_index("tile")
-    power = n & (n - 1) == 0
+    half = n // 2
+    far_tile = lax.rem(tile + half, n)
+    local = lax.rem(tile, half)
+    base_tile = tile - local
+    power = half & (half - 1) == 0
 
     def partner(d):
         if not power:
-            return lax.rem(n + d - tile, n)
+            return base_tile + lax.rem(half + d - local, half)
         other = tile
         bit = 1
-        while bit < n:
+        while bit < half:
             other = other + ((d // bit) % 2) * bit * (1 - 2 * ((tile // bit) % 2))
             bit *= 2
         return other
 
-    fetch_echo = pltpu.make_async_copy(echo_hbm, echo_ref, fetch_sems.at[0])
     fetches = [
-        pltpu.make_async_copy(table_hbm, table_ref, fetch_sems.at[1]),
-        pltpu.make_async_copy(phase_hbm, phase_ref, fetch_sems.at[2]),
+        pltpu.make_async_copy(starts_hbm, starts.at[NEAR], fetch_sems.at[0]),
+        pltpu.make_async_copy(phase_hbm, phase_ref.at[NEAR], fetch_sems.at[1]),
+        pltpu.make_async_copy(echo_hbm, got.at[0], fetch_sems.at[2]),
+        pltpu.make_async_copy(table_hbm, table_ref, fetch_sems.at[3]),
     ]
     barrier = pltpu.get_barrier_semaphore()
-    fetch_echo.start()
     for copy in fetches:
         copy.start()
     for d in range(1, groups):
@@ -143,49 +156,60 @@
             found = found | (lists_ref[strip, j] == number)
         return found
 
-    fetch_echo.wait()
-
-    def pick(d, c):
-        other = partner(d)
-        block = echo_ref[0]
-        for b in range(1, held):
-            block = jnp.where(names(other, tile * held + b), echo_ref[b], block)
-        picked[d] = block
-        return c
-
-    lax.fori_loop(0, n, pick, 0)
     pl.semaphore_wait(barrier, n - 1 + groups - 1)
 
-    def block_copy(d):
+    def remote(src, dst, send_sem, recv_sem, target):
         return pltpu.make_async_remote_copy(
-            src_ref=picked.at[d],
-            dst_ref=got.at[d],
-            send_sem=sends.at[d],
-            recv_sem=recvs.at[d],
-            device_id={"tile": partner(d)},
+            src_ref=src,
+            dst_ref=dst,
+            send_sem=send_sem,
+            recv_sem=recv_sem,
+            device_id=target,
             device_id_type=MESH,
         )
 
-    def send(i, c):
-        block_copy(n - i).start()
+    infos = [
+        remote(src, dst, info_sends.at[j], info_recvs.at[j], {"tile": far_tile})
+        for j, (src, dst) in enumerate(
+            ((starts_hbm, starts_far), (phase_hbm, phase_ref.at[FAR]))
+        )
+    ]
+    for copy in infos:
+        copy.start()
+
+    def block_copy(d):
+        return remote(echo_hbm, got.at[d], sends.at[d], recvs.at[d], {"tile": partner(d)})
+
+    def send(d, c):
+        block_copy(d).start()
         return c
 
-    lax.fori_loop(1, n, send, 0)
+    lax.fori_loop(1, half, send, 0)
 
     lane = lax.broadcasted_iota(jnp.int32, (8, 128), 1)
     sub = lax.broadcasted_iota(jnp.int32, (8, 128), 0)
     wide[:, bins:, :] = jnp.zeros((planes, wide.shape[1] - bins, 128), F32)
     acc[...] = jnp.zeros_like(acc)
+    strip_tile = (tile, far_tile)
     column_in_quad = (512 * sub + lane).astype(F32)
 
-    def widen(block):
-        wide[:, :bins, :] = block[: planes * bins].astype(F32).reshape(planes, bins, 128)
-
-    def gather(pair):
+    def chosen(strip, d, at):
+        number = partner(d) * held
+        block = got[d, 0, at]
+        for b in range(1, held):
+            block = jnp.where(names(strip_tile[strip], number + b), got[d, b, at], block)
+        return block
+
+    def widen(strip, d):
+        block = chosen(strip, d, slice(0, planes * bins))
+        wide[:, :bins, :] = block.astype(F32).reshape(planes, bins, 128)
+
+    def gather(strip, pair):
         for plane in range(planes):
             halves = []
             for h in range(2):
-                begin = start_ref[2 * pair + h]
+                row = 2 * pair + h
+                begin = starts[strip, row // 128, lax.rem(row, 128)]
                 at = begin // 128
                 off = begin - 128 * at
                 shift = lax.rem(128 - off, 128)
@@ -210,17 +234,18 @@
                 lhs[plane], table_ref[:, 256:512], preferred_element_type=F32
             )
 
-    def phase(d, tail):
-        source = partner(d)
-        used = names(tile, source * held)
+    def phase(strip, d):
+        tail = chosen(strip, d, slice(planes * bins, planes * bins + 16))
+        number = partner(d) * held
+        used = names(strip_tile[strip], number)
         for b in range(1, held):
-            used = used | names(tile, source * held + b)
+            used = used | names(strip_tile[strip], number + b)
         weight = jnp.where(used, 1.0, 0.0).astype(F32)
         tail = tail.astype(F32)
         for p in range(pulses):
             slope = tail[p : p + 1]
             shift = tail[pulses + p : pulses + p + 1]
-            turn_im, turn_re = sine_cosine(phase_ref[...] * shift)
+            turn_im, turn_re = sine_cosine(phase_ref[strip] * shift)
             rowturn[p, 0] = turn_re
             rowturn[p, 1] = turn_im
             im, re = sine_cosine(column_in_quad * slope)
@@ -232,7 +257,7 @@
                 ramp[p, 1, q] = im
                 re, im = re * step_re - im * step_im, re * step_im + im * step_re
 
-    def turn(pair):
+    def turn(strip, pair):
         rows_at = [2 * pair, 2 * pair + 1]
         row_turn = [
             [[rowturn[p, part_of, pl.ds(r, 1), :] for part_of in range(2)] for p in range(pulses)]
@@ -242,8 +267,8 @@
             ramps = [[ramp[p, part_of, q] for part_of in range(2)] for p in range(pulses)]
             for h, r in enumerate(rows_at):
                 at = pl.ds(pl.multiple_of(8 * r, 8), 8)
-                total_re = acc[0, r, q]
-                total_im = acc[1, r, q]
+                total_re = acc[strip, 0, r, q]
+                total_im = acc[strip, 1, r, q]
                 for p in range(pulses):
                     row_re, row_im = row_turn[h][p]
                     ramp_re, ramp_im = ramps[p]
@@ -253,104 +278,134 @@
                     value_im = product[2 * p + 1, at, 128 * q : 128 * q + 128]
                     total_re = total_re + (value_re * re - value_im * im)
                     total_im = total_im + (value_re * im + value_im * re)
-                acc[0, r, q] = total_re
-                acc[1, r, q] = total_im
-
-    def gather_only(pair, c):
-        gather(pair)
-        return c
-
-    def gather_and_turn(pair, c):
-        gather(pair)
-        turn(pair)
-        return c
-
-    def turn_only(pair, c):
-        turn(pair)
-        return c
-
-    tail_rows = slice(planes * bins, planes * bins + 16)
-    widen(picked[0])
-    lax.fori_loop(0, rows // 2, gather_only, 0, unroll=2)
-    for copy in fetches:
-        copy.wait()
-    multiply()
-    phase(0, picked[0, tail_rows])
-
-    def slot(d, c):
+                acc[strip, 0, r, q] = total_re
+                acc[strip, 1, r, q] = total_im
+
+    def rows_loop(gathered, turned):
+        def step(pair, c):
+            if gathered is not None:
+                gather(gathered, pair)
+            if turned is not None:
+                turn(turned, pair)
+            return c
+
+        lax.fori_loop(0, rows // 2, step, 0, unroll=2)
+
+    def arrive(d):
         block_copy(d).wait_recv()
-        widen(got[d])
-        lax.fori_loop(0, rows // 2, gather_and_turn, 0, unroll=2)
+
+    def finish(strip, d):
         multiply()
-        phase(d, got[d, tail_rows])
-        return c
-
-    lax.fori_loop(1, n, slot, 0)
-    lax.fori_loop(0, rows // 2, turn_only, 0, unroll=2)
-
-    def sent(d, c):
-        block_copy(d).wait_send()
-        return c
-
-    lax.fori_loop(1, n, sent, 0)
-
-    def place(r, c):
-        for plane in range(2):
-            for q in range(4):
-                image[pl.ds((plane * rows + r) * KBLOCKS + q, QUADS, stride=4), :] = (
-                    acc[plane, r, q] * scale
-                )
-        return c
-
-    lax.fori_loop(0, rows, place, 0, unroll=2)
+        phase(strip, d)
+
+    def part_copy(strip, d):
+        target = lax.rem(group + d, groups)
+        return remote(
+            part.at[strip, target],
+            got_part.at[strip, d - 1],
+            part_sends.at[strip, d - 1],
+            part_recvs.at[strip, d - 1],
+            {"pulse": target},
+        )
 
     together = 16 // share
     main = 2 * rows * share
     wide_lane = lax.broadcasted_iota(jnp.int32, (rows, 128), 1)
 
-    def emit_for(g):
-        def emit(i, c):
-            parts = [
-                image[pl.ds((i * together + h) * KBLOCKS + share * g, share), :]
-                for h in range(together)
-            ]
-            part[g, pl.ds(pl.multiple_of(16 * i, 16), 16), :] = jnp.concatenate(
-                parts, axis=0
-            ).astype(BF16)
+    def emit_strip(strip):
+        def place(r, c):
+            for plane in range(2):
+                for q in range(4):
+                    image[pl.ds((plane * rows + r) * KBLOCKS + q, QUADS, stride=4), :] = (
+                        acc[strip, plane, r, q] * scale
+                    )
             return c
 
-        lax.fori_loop(0, 2 * rows // together, emit, 0, unroll=4)
-        after = jnp.minimum(share * (g + 1), KBLOCKS - 1)
-        before = jnp.maximum(share * g - 1, 0)
-        for plane in range(2):
-            edge = jnp.where(
-                wide_lane < 64,
-                image[pl.ds(plane * rows * KBLOCKS + after, rows, stride=KBLOCKS), :],
-                image[pl.ds(plane * rows * KBLOCKS + before, rows, stride=KBLOCKS), :],
-            )
-            part[g, main + plane * rows : main + (plane + 1) * rows, :] = edge.astype(BF16)
-
-    copies = []
-    for d in range(groups - 1, 0, -1):
-        target = lax.rem(group + d, groups)
-        emit_for(target)
-        copy = pltpu.make_async_remote_copy(
-            src_ref=part.at[target],
-            dst_ref=got_part.at[d - 1],
-            send_sem=part_sends.at[d - 1],
-            recv_sem=part_recvs.at[d - 1],
-            device_id={"pulse": target},
-            device_id_type=MESH,
-        )
-        copy.start()
-        copies.append(copy)
-    emit_for(group)
-    for copy in copies:
+        lax.fori_loop(0, rows, place, 0, unroll=4)
+
+        def emit_for(g):
+            def emit(i, c):
+                parts = [
+                    image[pl.ds((i * together + h) * KBLOCKS + share * g, share), :]
+                    for h in range(together)
+                ]
+                part[strip, g, pl.ds(pl.multiple_of(16 * i, 16), 16), :] = jnp.concatenate(
+                    parts, axis=0
+                ).astype(BF16)
+                return c
+
+            lax.fori_loop(0, 2 * rows // together, emit, 0, unroll=4)
+            after = jnp.minimum(share * (g + 1), KBLOCKS - 1)
+            before = jnp.maximum(share * g - 1, 0)
+            for plane in range(2):
+                edge = jnp.where(
+                    wide_lane < 64,
+                    image[pl.ds(plane * rows * KBLOCKS + after, rows, stride=KBLOCKS), :],
+                    image[pl.ds(plane * rows * KBLOCKS + before, rows, stride=KBLOCKS), :],
+                )
+                part[strip, g, main + plane * rows : main + (plane + 1) * rows, :] = edge.astype(
+                    BF16
+                )
+
+        for d in range(groups - 1, 0, -1):
+            emit_for(lax.rem(group + d, groups))
+            part_copy(strip, d).start()
+        emit_for(group)
+
+    def summed(strip):
+        for d in range(1, groups):
+            part_copy(strip, d).wait_recv()
+        total = part[strip, group].astype(F32)
+        for d in range(1, groups):
+            total = total + got_part[strip, d - 1].astype(F32)
+        return total
+
+    for copy in fetches[:3]:
         copy.wait()
-
-    total = part[group].astype(F32)
-    for d in range(1, groups):
-        total = total + got_part[d - 1].astype(F32)
+    widen(NEAR, 0)
+    rows_loop(NEAR, None)
+    fetches[3].wait()
+    finish(NEAR, 0)
+
+    for copy in infos:
+        copy.wait_recv()
+    far_starts = pltpu.make_async_copy(starts_far, starts.at[FAR], fetch_sems.at[0])
+    far_starts.start()
+    widen(FAR, 0)
+    far_starts.wait()
+    rows_loop(FAR, NEAR)
+    finish(FAR, 0)
+
+    def far_slot(d, c):
+        arrive(d)
+        widen(FAR, d)
+        rows_loop(FAR, FAR)
+        finish(FAR, d)
+        return c
+
+    lax.fori_loop(1, half, far_slot, 0)
+
+    widen(NEAR, 1)
+    rows_loop(NEAR, FAR)
+    emit_strip(FAR)
+    finish(NEAR, 1)
+
+    def near_slot(d, c):
+        widen(NEAR, d)
+        rows_loop(NEAR, NEAR)
+        finish(NEAR, d)
+        return c
+
+    lax.fori_loop(2, half, near_slot, 0)
+    rows_loop(None, NEAR)
+    emit_strip(NEAR)
+
+    far_out[...] = summed(FAR).astype(BF16)
+    cross = remote(far_out, far_in, far_sends.at[0], far_recvs.at[0], {"tile": far_tile})
+    cross.start()
+    total = summed(NEAR)
+    cross.wait_recv()
+    total = total + far_in[...].astype(F32)
     for plane in range(2):
         first[plane, HALO : HALO + rows, 0:share, :] = total[
             plane * rows * share : (plane + 1) * rows * share
@@ -457,6 +512,18 @@
     sweep(first, 1, rows + 2 * HALO - 1, write_second)
     sweep(second, HALO, rows + HALO, write_out)
 
+    def sent(d, c):
+        block_copy(d).wait_send()
+        return c
+
+    lax.fori_loop(1, half, sent, 0)
+    for copy in infos:
+        copy.wait_send()
+    cross.wait_send()
+    for strip in (NEAR, FAR):
+        for d in range(1, groups):
+            part_copy(strip, d).wait_send()
+
 
 def body(echoes, pulse_slope, pulse_shift, footprint, band_start, row_phase):
     n = lax.axis_size("tile")
@@ -471,6 +538,8 @@
     values = jnp.broadcast_to(values[:, :, None], (held, 16, 128))
     message = jnp.concatenate([echoes.reshape(held, planes * bins, 128), values], axis=1)
     phases = jnp.broadcast_to(row_phase[:, None], (rows, 128))
+    start_rows = 8 * (-(-rows // 1024))
+    starts = jnp.pad(band_start, (0, 128 * start_rows - rows)).reshape(start_rows, 128)
     table = jnp.asarray(interpolation_table(), BF16)
 
     vmem = pl.BlockSpec(memory_space=pltpu.VMEM)
@@ -478,44 +547,49 @@
     anywhere = pl.BlockSpec(memory_space=pl.ANY)
     padded = -(-(share + 1) // 8) * 8
     extent = rows + 2 * HALO
-    slot = (planes * bins + 16, 128)
     piece = (2 * rows * share + 2 * rows, 128)
     dma = pltpu.SemaphoreType.DMA
     refined = pl.pallas_call(
         functools.partial(kernel, held, pulses, rows, groups, n),
         out_shape=jax.ShapeDtypeStruct((2, rows, share, 128), F32),
-        in_specs=[smem, smem, anywhere, anywhere, anywhere],
+        in_specs=[smem, anywhere, anywhere, anywhere, anywhere],
         out_specs=vmem,
         scratch_shapes=[
-            pltpu.VMEM(message.shape, BF16),
-            pltpu.VMEM(phases.shape, F32),
+            pltpu.VMEM(starts.shape, jnp.int32),
+            pltpu.SMEM((2,) + starts.shape, jnp.int32),
+            pltpu.VMEM((2,) + phases.shape, F32),
             pltpu.VMEM(table.shape, BF16),
-            dma((3,)),
-            pltpu.VMEM((n,) + slot, BF16),
-            pltpu.VMEM((n,) + slot, BF16),
+            pltpu.VMEM((n // 2,) + message.shape, BF16),
             pltpu.VMEM((planes, bins + 8, 128), F32),
             pltpu.VMEM((planes, rows * QUADS, 512), BF16),
             pltpu.VMEM((planes, rows * QUADS, 512), F32),
             pltpu.VMEM((pulses, 2, 4, 8, 128), F32),
             pltpu.VMEM((pulses, 2, rows, 128), F32),
-            pltpu.VMEM((2, rows, 4, 8, 128), F32),
+            pltpu.VMEM((2, 2, rows, 4, 8, 128), F32),
             pltpu.VMEM((2 * rows * KBLOCKS, 128), F32),
-            pltpu.VMEM((groups,) + piece, BF16),
-            pltpu.VMEM((groups - 1,) + piece, BF16),
+            pltpu.VMEM((2, groups) + piece, BF16),
+            pltpu.VMEM((2, groups - 1) + piece, BF16),
+            pltpu.VMEM(piece, BF16),
+            pltpu.VMEM(piece, BF16),
             pltpu.VMEM((2, extent, padded, 128), F32),
             pltpu.VMEM((2, extent, padded, 128), F32),
             pltpu.VMEM((2, 2, HALO, padded, 128), F32),
-            dma((n,)),
-            dma((n,)),
-            dma((groups - 1,)),
-            dma((groups - 1,)),
+            dma((4,)),
+            dma((2,)),
+            dma((2,)),
+            dma((n // 2,)),
+            dma((n // 2,)),
+            dma((2, groups - 1)),
+            dma((2, groups - 1)),
+            dma((1,)),
+            dma((1,)),
             dma((2,)),
             dma((2,)),
         ],
         compiler_params=pltpu.CompilerParams(
             collective_id=0, has_side_effects=True, vmem_limit_bytes=48 * 1024 * 1024
         ),
-    )(footprint[0], band_start, message, phases, table)
+    )(footprint[0], starts, message, phases, table)
     return refined.reshape(2, rows, NCOL // groups)
 
 

time: 58.5 us -> 50.3 us (0.86)
  Pallas kernels: 54.1 us -> 45.3 us
  local copies, waits for them, and re-layouts: 3.39 us -> 4 us
    pallas_call x1, Pallas kernels: 54.1 us -> 45.3 us  [body(): pl.pallas_call(functools.partial(kernel, held, pulses, rows, groups, n),...]
    unnamed x8, local copies, waits for them, and re-layouts: 1.29 us -> 1.9 us
where the time goes in v4:
time: 50.3 us; the launch traced here: 50.1 us
  Pallas kernels  45.3 us (90%)
  local copies, waits for them, and re-layouts  4 us (8%)
  other arithmetic  0.77 us (2%)
    pallas_call x1, Pallas kernels, body(): pl.pallas_call(functools.partial(kernel, held, pulses, rows, groups, n),...  45.3 us
    unnamed x8, local copies, waits for them, and re-layouts  1.9 us
    reshape x1, local copies, waits for them, and re-layouts, body(): echoes.reshape(held, planes * bins, 128)  1.21 us

profile of v4, /device:TPU:0, one launch (start us, length us, event | category | flops | bytes accessed | tf_op | source)
XLA Modules:
  0.0 50.1 jit_solution(16081392346997899357)
XLA Ops:
  0.0 0.0 copy-start
  0.0 1.2 %reshape.12 = bf16[2,512,128]{2,1,0:T(8,128)(2,1)S(1)} reshape(bf16[2,2,2,16384]{3,2,1,0:T(2,128)(2,1)} %param.7) | data formatting | bytes 524288 | tf_op jit(solution)/shard_map/reshape | solution.py:539
  1.2 0.8 %fusion.2 = bf16[2,16]{1,0:T(2,128)(2,1)S(1)} fusion(bf16[2,2]{1,0:T(2,128)(2,1)} %param.9, bf16[2,2]{1,0:T(2,128)(2,1)} %param.8), kind=kLoop, calls=%fused_computation.5 | loop fusion | flops 224 | bytes 80 | tf_op jit(solution)/shard_map/concatenate | solution.py:536
  2.0 0.1 broadcast_in_dim.4
  2.0 0.0 copy-start.2
  2.1 0.6 %copy-done.2 = f32[32]{0:T(128)S(1)} copy-done((f32[32]{0:T(128)S(1)}, f32[32]{0:T(128)}, u32[]{:S(2)}) %copy-start.2) | copy-done | bytes 152
  2.7 0.0 copy-start.3
  2.7 0.1 broadcast_in_dim.5.phase_hbm
  2.8 0.6 %copy-done.3 = s32[32]{0:T(128)S(1)} copy-done((s32[32]{0:T(128)S(1)}, s32[32]{0:T(128)}, u32[]{:S(2)}) %copy-start.3) | copy-done | bytes 152
  3.4 0.0 copy-start.1
  3.4 0.0 copy-done
  3.4 0.7 %copy-done.1 = s32[1,8,8]{2,1,0:T(8,128)S(1)} copy-done((s32[1,8,8]{2,1,0:T(8,128)S(1)}, s32[1,8,8]{2,1,0:T(8,128)}, u32[]{:S(2)}) %copy-start.1) | copy-done | bytes 280
  4.0 45.3 %shard_map.73 = f32[2,32,8,128]{3,2,1,0:T(8,128)S(1)} custom-call(s32[8,8]{1,0:T(8,128)S(1)} %bitcast.5, s32[8,128]{1,0:T(8,128)S(1)} %pad_bitcast_fusion.starts_hbm, bf16[2,528,128]{2,1,0:T(8,128)(2,1)S(1)} %pad_maximum_fusion.echo_hbm, f32[32,128]{1,0:T(8,128)S(1)} %broadcast_in_dim.5.phase_hbm, bf16[512,512]{1,0:T(8,128)(2,1)S(1)} %copy-done), custom_call_target="tpu_custom_call" | custom-call | tf_op jit(solution)/shard_map/pallas_call | solution.py:552
  49.3 0.7 %reshape.13 = f32[2,32,1024]{2,1,0:T(8,128)} reshape(f32[2,32,8,128]{3,2,1,0:T(8,128)S(1)} %shard_map.73) | data formatting | bytes 524288 | tf_op jit(solution)/shard_map/reshape | solution.py:593
  (2 shorter events, 0.0 us)
Async XLA Ops:
  0.0 3.4 %copy-start = (bf16[512,512]{1,0:T(8,128)(2,1)S(1)}, bf16[512,512]{1,0:T(8,128)(2,1)}, u32[]{:S(2)}) copy-start(bf16[512,512]{1,0:T(8,128)(2,1)} %constant.6.clone.table_hbm) | copy-start | bytes 1572868
  2.0 0.7 %copy-start.2 = (f32[32]{0:T(128)S(1)}, f32[32]{0:T(128)}, u32[]{:S(2)}) copy-start(f32[32]{0:T(128)} %param.12) | copy-start | bytes 388
  2.7 0.7 %copy-start.3 = (s32[32]{0:T(128)S(1)}, s32[32]{0:T(128)}, u32[]{:S(2)}) copy-start(s32[32]{0:T(128)} %param.11) | copy-start | bytes 388
  3.4 0.7 %copy-start.1 = (s32[1,8,8]{2,1,0:T(8,128)S(1)}, s32[1,8,8]{2,1,0:T(8,128)}, u32[]{:S(2)}) copy-start(s32[1,8,8]{2,1,0:T(8,128)} %param.10) | copy-start | bytes 772

commit v5 on v4

v5 whole, which is shorter than its diff:
```python
import functools

import jax
import jax.numpy as jnp
import numpy as np
from jax import lax
from jax.experimental import pallas as pl
from jax.experimental.pallas import tpu as pltpu
from jax.sharding import PartitionSpec as P

NCOL = 4096
ITERS = 2
KBLOCKS = NCOL // 128
QUADS = KBLOCKS // 4
HALO = ITERS

step_size = 0.5
tv_weight = 0.4
floor_square = 0.25

MESH = pl.DeviceIdType.MESH
F32 = jnp.float32
BF16 = jnp.bfloat16


def interpolation_table():
    columns = np.arange(128)
    position = 3 * columns + 4
    base = position // 4
    f = (position % 4) / 4.0
    weights = [
        (-(f**3) + 2 * f**2 - f) / 2,
        (3 * f**3 - 5 * f**2 + 2) / 2,
        (-3 * f**3 + 4 * f**2 + f) / 2,
        (f**3 - f**2) / 2,
    ]
    table = np.zeros((512, 512), np.float32)
    for q in range(4):
        for shift, weight in zip(range(-1, 3), weights):
            table[96 * q + base + shift, 128 * q + columns] += weight
    return table


def sine_cosine(angle):
    turns = jnp.floor(angle * 0.6366197723675814 + 0.5)
    rest = angle - turns * 1.5703125
    rest = rest - turns * 4.837512969970703125e-4
    rest = rest - turns * 7.549789948768648e-8
    square = rest * rest
    sine = rest + rest * square * (
        -1.6666654611e-1 + square * (8.3321608736e-3 - square * 1.9515295891e-4)
    )
    cosine = (1.0 - 0.5 * square) + square * square * (
        4.166664568298827e-2 + square * (-1.388731625493765e-3 + square * 2.443315711809948e-5)
    )
    quarter = turns - 4.0 * jnp.floor(turns * 0.25)
    odd = (quarter == 1.0) | (quarter == 3.0)
    sine_sign = jnp.where(quarter >= 2.0, -1.0, 1.0)
    cosine_sign = jnp.where((quarter == 1.0) | (quarter == 2.0), -1.0, 1.0)
    return (
        sine_sign * jnp.where(odd, cosine, sine),
        cosine_sign * jnp.where(odd, sine, cosine),
    )


NEAR, FAR = 0, 1


def kernel(
    held,
    pulses,
    rows,
    groups,
    n,
    lists_hbm,
    starts_hbm,
    echo_hbm,
    slope_hbm,
    shift_hbm,
    phase_hbm,
    table_hbm,
    out_ref,
    lists_ref,
    starts_far,
    starts,
    slope_ref,
    shift_ref,
    phase_line,
    phase_ref,
    table_ref,
    values,
    got_values,
    got,
    wide,
    lhs,
    product,
    ramp,
    rowturn,
    acc,
    part,
    got_part,
    far_out,
    far_in,
    first,
    second,
    halo_out,
    halo,
    fetch_sems,
    info_sends,
    info_recvs,
    sends,
    recvs,
    value_sends,
    value_recvs,
    part_sends,
    part_recvs,
    far_sends,
    far_recvs,
    halo_sends,
    halo_recvs,
):
    planes = 2 * pulses
    bins = echo_hbm.shape[1] // planes
    share = KBLOCKS // groups
    blocks = share + 1
    scale = float(pulses * n * groups) ** -0.5
    group = lax.axis_index("pulse")
    tile = lax.axis_index("tile")
    half = n // 2
    far_tile = lax.rem(tile + half, n)
    local = lax.rem(tile, half)
    base_tile = tile - local
    power = half & (half - 1) == 0

    def partner(d):
        if not power:
            return base_tile + lax.rem(half + d - local, half)
        other = tile
        bit = 1
        while bit < half:
            other = other + ((d // bit) % 2) * bit * (1 - 2 * ((tile // bit) % 2))
            bit *= 2
        return other

    fetches = [
        pltpu.make_async_copy(slope_hbm, slope_ref, fetch_sems.at[0]),
        pltpu.make_async_copy(shift_hbm, shift_ref, fetch_sems.at[1]),
        pltpu.make_async_copy(starts_hbm, starts.at[NEAR], fetch_sems.at[2]),
        pltpu.make_async_copy(phase_hbm, phase_line.at[NEAR], fetch_sems.at[3]),
        pltpu.make_async_copy(lists_hbm, lists_ref, fetch_sems.at[4]),
        pltpu.make_async_copy(echo_hbm, got.at[0], fetch_sems.at[5]),
        pltpu.make_async_copy(table_hbm, table_ref, fetch_sems.at[6]),
    ]
    barrier = pltpu.get_barrier_semaphore()
    for copy in fetches:
        copy.start()
    for d in range(1, groups):
        pl.semaphore_signal(
            barrier, inc=1, device_id={"pulse": lax.rem(group + d, groups)}, device_id_type=MESH
        )
    for d in range(1, n):
        pl.semaphore_signal(
            barrier, inc=1, device_id={"tile": lax.rem(tile + d, n)}, device_id_type=MESH
        )

    def names(strip, number):
        found = lists_ref[0, strip, 0] == number
        for j in range(1, lists_ref.shape[2]):
            found = found | (lists_ref[0, strip, j] == number)
        return found

    for copy in fetches[:2]:
        copy.wait()
    for b in range(held):
        for j, ref in enumerate((slope_ref, shift_ref)):
            for p in range(pulses):
                values[planes * b + pulses * j + p : planes * b + pulses * j + p + 1, :] = (
                    jnp.broadcast_to(ref[b : b + 1, p : p + 1].astype(F32), (1, 128))
                )
    pl.semaphore_wait(barrier, n - 1 + groups - 1)

    def remote(src, dst, send_sem, recv_sem, target):
        return pltpu.make_async_remote_copy(
            src_ref=src,
            dst_ref=dst,
            send_sem=send_sem,
            recv_sem=recv_sem,
            device_id=target,
            device_id_type=MESH,
        )

    infos = [
        remote(src, dst, info_sends.at[j], info_recvs.at[j], {"tile": far_tile})
        for j, (src, dst) in enumerate(
            ((starts_hbm, starts_far), (phase_hbm, phase_line.at[FAR]))
        )
    ]
    for copy in infos:
        copy.start()

    def block_copy(d):
        return remote(echo_hbm, got.at[d], sends.at[d], recvs.at[d], {"tile": partner(d)})

    def value_copy(d):
        return remote(
            values, got_values.at[d], value_sends.at[d], value_recvs.at[d], {"tile": partner(d)}
        )

    def send(d, c):
        block_copy(d).start()
        value_copy(d).start()
        return c

    lax.fori_loop(1, half, send, 0)

    lane = lax.broadcasted_iota(jnp.int32, (8, 128), 1)
    sub = lax.broadcasted_iota(jnp.int32, (8, 128), 0)
    wide[:, bins:, :] = jnp.zeros((planes, wide.shape[1] - bins, 128), F32)
    acc[...] = jnp.zeros_like(acc)
    strip_tile = (tile, far_tile)
    column_in_quad = (512 * sub + lane).astype(F32)

    def spread(strip):
        across = (rows, rows)
        diagonal = lax.broadcasted_iota(jnp.int32, across, 0) == lax.broadcasted_iota(
            jnp.int32, across, 1
        )
        line = jnp.where(diagonal, jnp.broadcast_to(phase_line[strip], across), 0.0)
        phase_ref[strip] = jnp.broadcast_to(jnp.sum(line, axis=1, keepdims=True), (rows, 128))

    def widen(strip, d):
        number = partner(d) * held
        block = got[d, 0]
        for b in range(1, held):
            block = jnp.where(names(strip_tile[strip], number + b), got[d, b], block)
        wide[:, :bins, :] = block.astype(F32).reshape(planes, bins, 128)

    def gather(strip, pair):
        for plane in range(planes):
            halves = []
            for h in range(2):
                row = 2 * pair + h
                begin = starts[strip, 0, row]
                at = begin // 128
                off = begin - 128 * at
                shift = lax.rem(128 - off, 128)
                keep = lane < 128 - off
                ys = [
                    pltpu.roll(wide[plane, pl.ds(at + o, 8, stride=3), :], shift, 1)
                    for o in range(5)
                ]
                halves.append([jnp.where(keep, ys[j], ys[j + 1]) for j in range(4)])
            for j in range(4):
                both = jnp.concatenate([halves[0][j], halves[1][j]], axis=0)
                lhs[plane, pl.ds(pl.multiple_of(16 * pair, 16), 16), 128 * j : 128 * j + 128] = (
                    both.astype(BF16)
                )

    def multiply():
        for plane in range(planes):
            product[plane, :, 0:256] = jnp.dot(
                lhs[plane, :, 0:256], table_ref[0:256, 0:256], preferred_element_type=F32
            )
            product[plane, :, 256:512] = jnp.dot(
                lhs[plane], table_ref[:, 256:512], preferred_element_type=F32
            )

    def phase(strip, d):
        number = partner(d) * held
        used = names(strip_tile[strip], number)
        tail = got_values[d, 0:planes]
        for b in range(1, held):
            named = names(strip_tile[strip], number + b)
            used = used | named
            tail = jnp.where(named, got_values[d, planes * b : planes * (b + 1)], tail)
        weight = jnp.where(used, 1.0, 0.0).astype(F32)
        for p in range(pulses):
            slope = tail[p : p + 1]
            shift = tail[pulses + p : pulses + p + 1]
            turn_im, turn_re = sine_cosine(phase_ref[strip] * shift)
            rowturn[p, 0] = turn_re
            rowturn[p, 1] = turn_im
            im, re = sine_cosine(column_in_quad * slope)
            step_im, step_re = sine_cosine(jnp.broadcast_to(128.0 * slope, (8, 128)))
            re = re * weight
            im = im * weight
            for q in range(4):
                ramp[p, 0, q] = re
                ramp[p, 1, q] = im
                re, im = re * step_re - im * step_im, re * step_im + im * step_re

    def acc_base(strip, plane):
        return (2 * strip + plane) * rows * KBLOCKS

    def turn(strip, pair):
        rows_at = [2 * pair, 2 * pair + 1]
        row_turn = [
            [[rowturn[p, part_of, pl.ds(r, 1), :] for part_of in range(2)] for p in range(pulses)]
            for r in rows_at
        ]
        for q in range(4):
            ramps = [[ramp[p, part_of, q] for part_of in range(2)] for p in range(pulses)]
            for h, r in enumerate(rows_at):
                at = pl.ds(pl.multiple_of(8 * r, 8), 8)
                at_re = pl.ds(pl.multiple_of(acc_base(strip, 0) + KBLOCKS * r + 8 * q, 8), 8)
                at_im = pl.ds(pl.multiple_of(acc_base(strip, 1) + KBLOCKS * r + 8 * q, 8), 8)
                total_re = acc[at_re, :]
                total_im = acc[at_im, :]
                for p in range(pulses):
                    row_re, row_im = row_turn[h][p]
                    ramp_re, ramp_im = ramps[p]
                    re = ramp_re * row_re - ramp_im * row_im
                    im = ramp_re * row_im + ramp_im * row_re
                    value_re = product[2 * p, at, 128 * q : 128 * q + 128]
                    value_im = product[2 * p + 1, at, 128 * q : 128 * q + 128]
                    total_re = total_re + (value_re * re - value_im * im)
                    total_im = total_im + (value_re * im + value_im * re)
                acc[at_re, :] = total_re
                acc[at_im, :] = total_im

    def rows_loop(gathered, turned):
        def step(pair, c):
            if gathered is not None:
                gather(gathered, pair)
            if turned is not None:
                turn(turned, pair)
            return c

        lax.fori_loop(0, rows // 2, step, 0, unroll=2)

    def arrive(d):
        value_copy(d).wait_recv()
        block_copy(d).wait_recv()

    def finish(strip, d):
        multiply()
        phase(strip, d)

    def part_copy(strip, d):
        target = lax.rem(group + d, groups)
        return remote(
            part.at[strip, target],
            got_part.at[strip, d - 1],
            part_sends.at[strip, d - 1],
            part_recvs.at[strip, d - 1],
            {"pulse": target},
        )

    wide_lane = lax.broadcasted_iota(jnp.int32, (rows, 128), 1)

    def column_block(strip, plane, k):
        start = acc_base(strip, plane) + QUADS * lax.rem(k, 4) + k // 4
        return acc[pl.ds(start, rows, stride=KBLOCKS), :] * scale

    def emit_strip(strip):
        def emit_for(g):
            for plane in range(2):
                for k in range(blocks):
                    if k < share:
                        value = column_block(strip, plane, share * g + k)
                    else:
                        value = jnp.where(
                            wide_lane < 64,
                            column_block(
                                strip, plane, jnp.minimum(share * (g + 1), KBLOCKS - 1)
                            ),
                            column_block(strip, plane, jnp.maximum(share * g - 1, 0)),
                        )
                    at = (plane * blocks + k) * rows
                    part[strip, g, at : at + rows, :] = value.astype(BF16)

        for d in range(groups - 1, 0, -1):
            emit_for(lax.rem(group + d, groups))
            part_copy(strip, d).start()
        emit_for(group)

    def summed(strip):
        for d in range(1, groups):
            part_copy(strip, d).wait_recv()
        total = part[strip, group].astype(F32)
        for d in range(1, groups):
            total = total + got_part[strip, d - 1].astype(F32)
        return total

    for copy in fetches[2:6]:
        copy.wait()
    spread(NEAR)
    got_values[0] = values[...]
    widen(NEAR, 0)
    rows_loop(NEAR, None)
    fetches[6].wait()
    finish(NEAR, 0)

    for copy in infos:
        copy.wait_recv()
    far_starts = pltpu.make_async_copy(starts_far, starts.at[FAR], fetch_sems.at[0])
    far_starts.start()
    spread(FAR)
    widen(FAR, 0)
    far_starts.wait()
    rows_loop(FAR, NEAR)
    finish(FAR, 0)

    def far_slot(d, c):
        arrive(d)
        widen(FAR, d)
        rows_loop(FAR, FAR)
        finish(FAR, d)
        return c

    lax.fori_loop(1, half, far_slot, 0)

    widen(NEAR, 1)
    rows_loop(NEAR, FAR)
    emit_strip(FAR)
    finish(NEAR, 1)

    def near_slot(d, c):
        widen(NEAR, d)
        rows_loop(NEAR, NEAR)
        finish(NEAR, d)
        return c

    lax.fori_loop(2, half, near_slot, 0)
    rows_loop(None, NEAR)
    emit_strip(NEAR)

    far_out[...] = summed(FAR).astype(BF16)
    cross = remote(far_out, far_in, far_sends.at[0], far_recvs.at[0], {"tile": far_tile})
    cross.start()
    total = summed(NEAR)
    cross.wait_recv()
    total = total + far_in[...].astype(F32)
    tall = rows + 16
    for i in range(2 * blocks):
        first[tall * i + 8 : tall * i + 8 + rows, :] = total[i * rows : (i + 1) * rows]
    for i in range(HALO):
        halo_out[1, i, 0 : 2 * blocks, :] = first[pl.ds(8 + i, 2 * blocks, stride=tall), :]
        halo_out[0, i, 0 : 2 * blocks, :] = first[
            pl.ds(8 + rows - HALO + i, 2 * blocks, stride=tall), :
        ]

    upward = remote(
        halo_out.at[1], halo.at[1], halo_sends.at[1], halo_recvs.at[1], {"tile": tile - 1}
    )
    downward = remote(
        halo_out.at[0], halo.at[0], halo_sends.at[0], halo_recvs.at[0], {"tile": tile + 1}
    )

    def put_halo(side, from_halo):
        for i in range(HALO):
            at = 8 - HALO + i if side == 0 else 8 + rows + i
            value = halo[side, i, 0 : 2 * blocks, :]
            if not from_halo:
                value = jnp.zeros_like(value)
            first[pl.ds(at, 2 * blocks, stride=tall), :] = value

    @pl.when(tile > 0)
    def _():
        upward.start()

    @pl.when(tile < n - 1)
    def _():
        downward.start()

    @pl.when(tile > 0)
    def _():
        downward.wait_recv()
        put_halo(0, True)

    @pl.when(tile == 0)
    def _():
        put_halo(0, False)

    @pl.when(tile < n - 1)
    def _():
        upward.wait_recv()
        put_halo(1, True)

    @pl.when(tile == n - 1)
    def _():
        put_halo(1, False)

    row = tile * rows - 8 + lax.broadcasted_iota(jnp.int32, (tall, 128), 0)
    line = lax.broadcasted_iota(jnp.int32, (1, 128), 1)
    tall_lane = lax.broadcasted_iota(jnp.int32, (tall, 128), 1)
    row_inside = (row >= 0) & (row < n * rows)
    row_down = (row >= 0) & (row < n * rows - 1)

    def sweep(source, write):
        field = [[source[tall * (p * blocks + k) : tall * (p * blocks + k + 1), :] for k in range(blocks)] for p in range(2)]
        down = [[], []]
        right = [[], []]
        for k in range(blocks):
            column = (group * share + k) * 128 + line
            if k == share:
                column = jnp.where(line < 64, column, column - 128 * blocks)
            column_inside = (column >= 0) & (column < NCOL)
            column_right = (column >= 0) & (column < NCOL - 1)
            square = floor_square
            for p in range(2):
                here = field[p][k]
                following = field[p][(k + 1) % blocks]
                beside = pltpu.roll(jnp.where(tall_lane == 0, following, here), 127, 1)
                below = pltpu.roll(here, tall - 1, 0)
                down[p].append(jnp.where(row_down & column_inside, below - here, 0.0))
                right[p].append(jnp.where(row_inside & column_right, beside - here, 0.0))
                square = square + (down[p][k] * down[p][k] + right[p][k] * right[p][k])
            inverse = lax.rsqrt(square)
            for p in range(2):
                down[p][k] = down[p][k] * inverse
                right[p][k] = right[p][k] * inverse
        for p in range(2):
            for k in range(blocks):
                before = right[p][(k - 1) % blocks]
                left = pltpu.roll(jnp.where(tall_lane == 127, before, right[p][k]), 1, 1)
                above = pltpu.roll(down[p][k], 1, 0)
                divergence = down[p][k] - above + right[p][k] - left
                at = tall * (p * blocks + k)
                here = field[p][k]
                base = first[at : at + tall, :]
                write(p, k, here - step_size * (here - base - tv_weight * divergence))

    def write_second(p, k, value):
        at = tall * (p * blocks + k)
        second[at : at + tall, :] = value

    def write_out(p, k, value):
        if k < share:
            out_ref[p, :, 128 * k : 128 * (k + 1)] = value[8 : 8 + rows]

    sweep(first, write_second)
    sweep(second, write_out)

    @pl.when(tile > 0)
    def _():
        upward.wait_send()

    @pl.when(tile < n - 1)
    def _():
        downward.wait_send()

    def sent(d, c):
        block_copy(d).wait_send()
        value_copy(d).wait_send()
        return c

    lax.fori_loop(1, half, sent, 0)
    for copy in infos:
        copy.wait_send()
    cross.wait_send()
    for strip in (NEAR, FAR):
        for d in range(1, groups):
            part_copy(strip, d).wait_send()


def body(echoes, pulse_slope, pulse_shift, footprint, band_start, row_phase):
    n = lax.axis_size("tile")
    groups = lax.axis_size("pulse")
    held, pulses = pulse_slope.shape
    rows = band_start.shape[0]
    bins = echoes.shape[3] // 128
    planes = 2 * pulses
    share = KBLOCKS // groups
    planes_of = echoes.reshape(held, planes * bins, 128)
    table = jnp.asarray(interpolation_table(), BF16)

    vmem = pl.BlockSpec(memory_space=pltpu.VMEM)
    anywhere = pl.BlockSpec(memory_space=pl.ANY)
    blocks = share + 1
    edge_rows = 8 * (-(-2 * blocks // 8))
    value_rows = 8 * (-(-held * planes // 8))
    field = (2 * blocks * (rows + 16), 128)
    piece = (2 * blocks * rows, 128)
    dma = pltpu.SemaphoreType.DMA
    refined = pl.pallas_call(
        functools.partial(kernel, held, pulses, rows, groups, n),
        out_shape=jax.ShapeDtypeStruct((2, rows, 128 * share), F32),
        in_specs=[anywhere] * 7,
        out_specs=vmem,
        scratch_shapes=[
            pltpu.SMEM(footprint.shape, jnp.int32),
            pltpu.VMEM((1, rows), jnp.int32),
            pltpu.SMEM((2, 1, rows), jnp.int32),
            pltpu.VMEM(pulse_slope.shape, BF16),
            pltpu.VMEM(pulse_shift.shape, BF16),
            pltpu.VMEM((2, 1, rows), F32),
            pltpu.VMEM((2, rows, 128), F32),
            pltpu.VMEM(table.shape, BF16),
            pltpu.VMEM((value_rows, 128), F32),
            pltpu.VMEM((n // 2, value_rows, 128), F32),
            pltpu.VMEM((n // 2,) + planes_of.shape, BF16),
            pltpu.VMEM((planes, bins + 8, 128), F32),
            pltpu.VMEM((planes, rows * QUADS, 512), BF16),
            pltpu.VMEM((planes, rows * QUADS, 512), F32),
            pltpu.VMEM((pulses, 2, 4, 8, 128), F32),
            pltpu.VMEM((pulses, 2, rows, 128), F32),
            pltpu.VMEM((4 * rows * KBLOCKS, 128), F32),
            pltpu.VMEM((2, groups) + piece, BF16),
            pltpu.VMEM((2, groups - 1) + piece, BF16),
            pltpu.VMEM(piece, BF16),
            pltpu.VMEM(piece, BF16),
            pltpu.VMEM(field, F32),
            pltpu.VMEM(field, F32),
            pltpu.VMEM((2, HALO, edge_rows, 128), F32),
            pltpu.VMEM((2, HALO, edge_rows, 128), F32),
            dma((7,)),
            dma((2,)),
            dma((2,)),
            dma((n // 2,)),
            dma((n // 2,)),
            dma((n // 2,)),
            dma((n // 2,)),
            dma((2, groups - 1)),
            dma((2, groups - 1)),
            dma((1,)),
            dma((1,)),
            dma((2,)),
            dma((2,)),
        ],
        compiler_params=pltpu.CompilerParams(
            collective_id=0, has_side_effects=True, vmem_limit_bytes=60 * 1024 * 1024
        ),
    )(
        footprint,
        band_start.reshape(1, rows),
        planes_of,
        pulse_slope,
        pulse_shift,
        row_phase.reshape(1, rows),
        table,
    )
    return refined


def solution(mesh):
    in_specs = (
        P(("pulse", "tile"), None, None, None),
        P(("pulse", "tile"), None),
        P(("pulse", "tile"), None),
        P("pulse", None, None),
        P("tile"),
        P("tile"),
    )
    out_specs = P(None, "tile", "pulse")
    return jax.shard_map(body, mesh=mesh, in_specs=in_specs, out_specs=out_specs, check_vma=False)
```

time: 50.3 us -> 47.4 us (0.942)
  Pallas kernels: 45.3 us -> 43.7 us
  other arithmetic: 0.77 us -> 0 us
    pallas_call x1, Pallas kernels: 45.3 us -> 43.7 us  [body(): pl.pallas_call(functools.partial(kernel, held, pulses, rows, groups, n),...]
    concatenate x2 -> x0, other arithmetic: 0.77 us -> none  [the longest x1 0.75 us: body(): values = jnp.concatenate([pulse_slope, pulse_shift], axis=1)]
    unnamed x8 -> x1, local copies, waits for them, and re-layouts: 1.9 us -> 1.67 us
    reshape x3 -> x1, local copies, waits for them, and re-layouts: 1.96 us -> 1.85 us  [body(): planes_of = echoes.reshape(held, planes * bins, 128)]
where the time goes in v5:
time: 47.4 us; the launch traced here: 47.3 us
  Pallas kernels  43.7 us (92%)
  local copies, waits for them, and re-layouts  3.53 us (7%)
    pallas_call x1, Pallas kernels, body(): pl.pallas_call(functools.partial(kernel, held, pulses, rows, groups, n),...  43.7 us
    reshape x1, local copies, waits for them, and re-layouts, body(): planes_of = echoes.reshape(held, planes * bins, 128)  1.85 us
    unnamed x1, local copies, waits for them, and re-layouts  1.67 us

profile of v5, /device:TPU:0, one launch (start us, length us, event | category | flops | bytes accessed | tf_op | source)
XLA Modules:
  0.0 47.3 jit_solution(17537571691003378141)
XLA Ops:
  0.0 1.9 %reshape.10.echo_hbm = bf16[2,512,128]{2,1,0:T(8,128)(2,1)} reshape(bf16[2,2,2,16384]{3,2,1,0:T(2,128)(2,1)} %param.7) | data formatting | bytes 524288 | tf_op jit(solution)/shard_map/reshape | solution.py:565
  1.9 43.7 %shard_map.73 = f32[2,32,1024]{2,1,0:T(8,128)} custom-call(s32[1,8,8]{2,1,0:T(8,128)} %lists_hbm.1, s32[1,32]{1,0:T(1,128)} %bitcast.2, bf16[2,512,128]{2,1,0:T(8,128)(2,1)} %reshape.10.echo_hbm, bf16[2,2]{1,0:T(2,128)(2,1)} %slope_hbm.1, bf16[2,2]{1,0:T(2,128)(2,1)} %shift_hbm.1, f32[1,32]{1,0:T(1,128)} %bitcast.3, bf16[512,512]{1,0:T(8,128)(2,1)} %constant.2.clone.table_hbm), custom_call_target="tpu_custom_call" | custom-call | tf_op jit(solution)/shard_map/pallas_call | solution.py:576
  45.6 1.7 %copy.9 = f32[2,32,1024]{2,1,0:T(8,128)} copy(f32[2,32,1024]{2,1,0:T(8,128)} %shard_map.73) | data formatting | bytes 524288

commit v6 on v5

--- a/solution.py
+++ b/solution.py
@@ -216,9 +216,12 @@
     lane = lax.broadcasted_iota(jnp.int32, (8, 128), 1)
     sub = lax.broadcasted_iota(jnp.int32, (8, 128), 0)
     wide[:, bins:, :] = jnp.zeros((planes, wide.shape[1] - bins, 128), F32)
-    acc[...] = jnp.zeros_like(acc)
-    strip_tile = (tile, far_tile)
+    for ref in (acc, lhs, product, ramp, rowturn):
+        ref[...] = jnp.zeros_like(ref)
     column_in_quad = (512 * sub + lane).astype(F32)
+
+    def tile_of(strip):
+        return jnp.where(strip == FAR, far_tile, tile)
 
     def spread(strip):
         across = (rows, rows)
@@ -232,45 +235,45 @@
         number = partner(d) * held
         block = got[d, 0]
         for b in range(1, held):
-            block = jnp.where(names(strip_tile[strip], number + b), got[d, b], block)
+            block = jnp.where(names(tile_of(strip), number + b), got[d, b], block)
         wide[:, :bins, :] = block.astype(F32).reshape(planes, bins, 128)
 
-    def gather(strip, pair):
-        for plane in range(planes):
-            halves = []
-            for h in range(2):
-                row = 2 * pair + h
-                begin = starts[strip, 0, row]
-                at = begin // 128
-                off = begin - 128 * at
-                shift = lax.rem(128 - off, 128)
-                keep = lane < 128 - off
-                ys = [
-                    pltpu.roll(wide[plane, pl.ds(at + o, 8, stride=3), :], shift, 1)
-                    for o in range(5)
-                ]
-                halves.append([jnp.where(keep, ys[j], ys[j + 1]) for j in range(4)])
-            for j in range(4):
-                both = jnp.concatenate([halves[0][j], halves[1][j]], axis=0)
-                lhs[plane, pl.ds(pl.multiple_of(16 * pair, 16), 16), 128 * j : 128 * j + 128] = (
-                    both.astype(BF16)
-                )
-
-    def multiply():
-        for plane in range(planes):
-            product[plane, :, 0:256] = jnp.dot(
-                lhs[plane, :, 0:256], table_ref[0:256, 0:256], preferred_element_type=F32
-            )
-            product[plane, :, 256:512] = jnp.dot(
-                lhs[plane], table_ref[:, 256:512], preferred_element_type=F32
-            )
+    def gather(strip, chunk):
+        side = chunk % 2
+        for pair in range(4):
+            for plane in range(planes):
+                halves = []
+                for h in range(2):
+                    begin = starts[strip, 0, 8 * chunk + 2 * pair + h]
+                    at = begin // 128
+                    off = begin - 128 * at
+                    shift = lax.rem(128 - off, 128)
+                    keep = lane < 128 - off
+                    ys = [
+                        pltpu.roll(wide[plane, pl.ds(at + o, 8, stride=3), :], shift, 1)
+                        for o in range(5)
+                    ]
+                    halves.append([jnp.where(keep, ys[j], ys[j + 1]) for j in range(4)])
+                for j in range(4):
+                    both = jnp.concatenate([halves[0][j], halves[1][j]], axis=0)
+                    at_row = 64 * plane + 16 * pair
+                    lhs[side, at_row : at_row + 16, 128 * j : 128 * j + 128] = both.astype(BF16)
+
+    def multiply(chunk):
+        side = chunk % 2
+        product[side, :, 0:256] = jnp.dot(
+            lhs[side, :, 0:256], table_ref[0:256, 0:256], preferred_element_type=F32
+        )
+        product[side, :, 256:512] = jnp.dot(
+            lhs[side], table_ref[:, 256:512], preferred_element_type=F32
+        )
 
     def phase(strip, d):
         number = partner(d) * held
-        used = names(strip_tile[strip], number)
+        used = names(tile_of(strip), number)
         tail = got_values[d, 0:planes]
         for b in range(1, held):
-            named = names(strip_tile[strip], number + b)
+            named = names(tile_of(strip), number + b)
             used = used | named
             tail = jnp.where(named, got_values[d, planes * b : planes * (b + 1)], tail)
         weight = jnp.where(used, 1.0, 0.0).astype(F32)
@@ -292,49 +295,39 @@
     def acc_base(strip, plane):
         return (2 * strip + plane) * rows * KBLOCKS
 
-    def turn(strip, pair):
-        rows_at = [2 * pair, 2 * pair + 1]
+    def turn(strip, chunk):
+        side = chunk % 2
         row_turn = [
-            [[rowturn[p, part_of, pl.ds(r, 1), :] for part_of in range(2)] for p in range(pulses)]
-            for r in rows_at
+            [
+                [rowturn[p, part_of, 8 * chunk + r : 8 * chunk + r + 1, :] for part_of in range(2)]
+                for p in range(pulses)
+            ]
+            for r in range(8)
         ]
         for q in range(4):
             ramps = [[ramp[p, part_of, q] for part_of in range(2)] for p in range(pulses)]
-            for h, r in enumerate(rows_at):
-                at = pl.ds(pl.multiple_of(8 * r, 8), 8)
-                at_re = pl.ds(pl.multiple_of(acc_base(strip, 0) + KBLOCKS * r + 8 * q, 8), 8)
-                at_im = pl.ds(pl.multiple_of(acc_base(strip, 1) + KBLOCKS * r + 8 * q, 8), 8)
+            for r in range(8):
+                at_row = KBLOCKS * (8 * chunk + r) + 8 * q
+                at_re = pl.ds(pl.multiple_of(acc_base(strip, 0) + at_row, 8), 8)
+                at_im = pl.ds(pl.multiple_of(acc_base(strip, 1) + at_row, 8), 8)
                 total_re = acc[at_re, :]
                 total_im = acc[at_im, :]
                 for p in range(pulses):
-                    row_re, row_im = row_turn[h][p]
+                    row_re, row_im = row_turn[r][p]
                     ramp_re, ramp_im = ramps[p]
                     re = ramp_re * row_re - ramp_im * row_im
                     im = ramp_re * row_im + ramp_im * row_re
-                    value_re = product[2 * p, at, 128 * q : 128 * q + 128]
-                    value_im = product[2 * p + 1, at, 128 * q : 128 * q + 128]
+                    at = 128 * p + 8 * r
+                    value_re = product[side, at : at + 8, 128 * q : 128 * q + 128]
+                    value_im = product[side, at + 64 : at + 72, 128 * q : 128 * q + 128]
                     total_re = total_re + (value_re * re - value_im * im)
                     total_im = total_im + (value_re * im + value_im * re)
                 acc[at_re, :] = total_re
                 acc[at_im, :] = total_im
 
-    def rows_loop(gathered, turned):
-        def step(pair, c):
-            if gathered is not None:
-                gather(gathered, pair)
-            if turned is not None:
-                turn(turned, pair)
-            return c
-
-        lax.fori_loop(0, rows // 2, step, 0, unroll=2)
-
     def arrive(d):
         value_copy(d).wait_recv()
         block_copy(d).wait_recv()
-
-    def finish(strip, d):
-        multiply()
-        phase(strip, d)
 
     def part_copy(strip, d):
         target = lax.rem(group + d, groups)
@@ -386,43 +379,49 @@
         copy.wait()
     spread(NEAR)
     got_values[0] = values[...]
-    widen(NEAR, 0)
-    rows_loop(NEAR, None)
     fetches[6].wait()
-    finish(NEAR, 0)
-
-    for copy in infos:
-        copy.wait_recv()
+    chunks = rows // 8
     far_starts = pltpu.make_async_copy(starts_far, starts.at[FAR], fetch_sems.at[0])
-    far_starts.start()
-    spread(FAR)
-    widen(FAR, 0)
-    far_starts.wait()
-    rows_loop(FAR, NEAR)
-    finish(FAR, 0)
-
-    def far_slot(d, c):
-        arrive(d)
-        widen(FAR, d)
-        rows_loop(FAR, FAR)
-        finish(FAR, d)
+
+    def place_of(i):
+        far = (i >= 1) & (i <= half)
+        d = jnp.where(far, i - 1, jnp.where(i > half, i - half, 0))
+        return jnp.where(far, FAR, NEAR), d
+
+    def slot(i, c):
+        strip, d = place_of(i)
+        last_strip, _ = place_of(i - 1)
+
+        @pl.when(i == 1)
+        def _():
+            for copy in infos:
+                copy.wait_recv()
+            far_starts.start()
+            spread(FAR)
+            far_starts.wait()
+
+        @pl.when((i >= 2) & (i <= half))
+        def _():
+            arrive(d)
+
+        widen(strip, d)
+        for chunk in range(chunks):
+            gather(strip, chunk)
+            multiply((chunk - 1) % chunks)
+            if chunk < 2:
+                turn(last_strip, (chunk - 2) % chunks)
+            else:
+                turn(strip, chunk - 2)
+            if chunk == 1:
+                phase(strip, d)
         return c
 
-    lax.fori_loop(1, half, far_slot, 0)
-
-    widen(NEAR, 1)
-    rows_loop(NEAR, FAR)
+    lax.fori_loop(0, half + 2, slot, 0)
     emit_strip(FAR)
-    finish(NEAR, 1)
-
-    def near_slot(d, c):
-        widen(NEAR, d)
-        rows_loop(NEAR, NEAR)
-        finish(NEAR, d)
-        return c
-
-    lax.fori_loop(2, half, near_slot, 0)
-    rows_loop(None, NEAR)
+    lax.fori_loop(half + 2, n, slot, 0)
+    multiply(chunks - 1)
+    turn(NEAR, chunks - 2)
+    turn(NEAR, chunks - 1)
     emit_strip(NEAR)
 
     far_out[...] = summed(FAR).astype(BF16)
@@ -591,8 +590,8 @@
             pltpu.VMEM((n // 2, value_rows, 128), F32),
             pltpu.VMEM((n // 2,) + planes_of.shape, BF16),
             pltpu.VMEM((planes, bins + 8, 128), F32),
-            pltpu.VMEM((planes, rows * QUADS, 512), BF16),
-            pltpu.VMEM((planes, rows * QUADS, 512), F32),
+            pltpu.VMEM((2, planes * 64, 512), BF16),
+            pltpu.VMEM((2, planes * 64, 512), F32),
             pltpu.VMEM((pulses, 2, 4, 8, 128), F32),
             pltpu.VMEM((pulses, 2, rows, 128), F32),
             pltpu.VMEM((4 * rows * KBLOCKS, 128), F32),

time: 47.4 us -> 45.9 us (0.968)
  Pallas kernels: 43.7 us -> 42.2 us
    pallas_call x1, Pallas kernels: 43.7 us -> 42.2 us  [body(): pl.pallas_call(functools.partial(kernel, held, pulses, rows, groups, n),...]
where the time goes in v6:
time: 45.9 us; the launch traced here: 45.7 us
  Pallas kernels  42.2 us (92%)
  local copies, waits for them, and re-layouts  3.53 us (8%)
    pallas_call x1, Pallas kernels, body(): pl.pallas_call(functools.partial(kernel, held, pulses, rows, groups, n),...  42.2 us
    reshape x1, local copies, waits for them, and re-layouts, body(): planes_of = echoes.reshape(held, planes * bins, 128)  1.85 us
    unnamed x1, local copies, waits for them, and re-layouts  1.67 us

profile of v6, /device:TPU:0, one launch (start us, length us, event | category | flops | bytes accessed | tf_op | source)
XLA Modules:
  0.0 45.7 jit_solution(17755210274242453958)
XLA Ops:
  0.0 1.9 %reshape.10.echo_hbm = bf16[2,512,128]{2,1,0:T(8,128)(2,1)} reshape(bf16[2,2,2,16384]{3,2,1,0:T(2,128)(2,1)} %param.7) | data formatting | bytes 524288 | tf_op jit(solution)/shard_map/reshape | solution.py:564
  1.9 42.2 %shard_map.73 = f32[2,32,1024]{2,1,0:T(8,128)} custom-call(s32[1,8,8]{2,1,0:T(8,128)} %lists_hbm.1, s32[1,32]{1,0:T(1,128)} %bitcast.2, bf16[2,512,128]{2,1,0:T(8,128)(2,1)} %reshape.10.echo_hbm, bf16[2,2]{1,0:T(2,128)(2,1)} %slope_hbm.1, bf16[2,2]{1,0:T(2,128)(2,1)} %shift_hbm.1, f32[1,32]{1,0:T(1,128)} %bitcast.3, bf16[512,512]{1,0:T(8,128)(2,1)} %constant.2.clone.table_hbm), custom_call_target="tpu_custom_call" | custom-call | tf_op jit(solution)/shard_map/pallas_call | solution.py:575
  44.0 1.7 %copy.9 = f32[2,32,1024]{2,1,0:T(8,128)} copy(f32[2,32,1024]{2,1,0:T(8,128)} %shard_map.73) | data formatting | bytes 524288

commit v7 on v6

--- a/solution.py
+++ b/solution.py
@@ -329,50 +329,50 @@
         value_copy(d).wait_recv()
         block_copy(d).wait_recv()
 
-    def part_copy(strip, d):
+    half_rows = rows // 2
+
+    def part_copy(strip, d, side):
         target = lax.rem(group + d, groups)
         return remote(
-            part.at[strip, target],
-            got_part.at[strip, d - 1],
-            part_sends.at[strip, d - 1],
-            part_recvs.at[strip, d - 1],
+            part.at[strip, target, side],
+            got_part.at[strip, d - 1, side],
+            part_sends.at[strip, d - 1, side],
+            part_recvs.at[strip, d - 1, side],
             {"pulse": target},
         )
 
-    wide_lane = lax.broadcasted_iota(jnp.int32, (rows, 128), 1)
-
-    def column_block(strip, plane, k):
-        start = acc_base(strip, plane) + QUADS * lax.rem(k, 4) + k // 4
-        return acc[pl.ds(start, rows, stride=KBLOCKS), :] * scale
-
-    def emit_strip(strip):
-        def emit_for(g):
-            for plane in range(2):
-                for k in range(blocks):
-                    if k < share:
-                        value = column_block(strip, plane, share * g + k)
-                    else:
-                        value = jnp.where(
-                            wide_lane < 64,
-                            column_block(
-                                strip, plane, jnp.minimum(share * (g + 1), KBLOCKS - 1)
-                            ),
-                            column_block(strip, plane, jnp.maximum(share * g - 1, 0)),
-                        )
-                    at = (plane * blocks + k) * rows
-                    part[strip, g, at : at + rows, :] = value.astype(BF16)
-
+    wide_lane = lax.broadcasted_iota(jnp.int32, (half_rows, 128), 1)
+
+    def emit_for(strip, side, g):
+        def column_block(plane, k):
+            start = acc_base(strip, plane) + side * half_rows * KBLOCKS
+            start = start + QUADS * lax.rem(k, 4) + k // 4
+            return acc[pl.ds(start, half_rows, stride=KBLOCKS), :] * scale
+
+        for plane in range(2):
+            for k in range(blocks):
+                if k < share:
+                    value = column_block(plane, share * g + k)
+                else:
+                    value = jnp.where(
+                        wide_lane < 64,
+                        column_block(plane, jnp.minimum(share * (g + 1), KBLOCKS - 1)),
+                        column_block(plane, jnp.maximum(share * g - 1, 0)),
+                    )
+                at = (plane * blocks + k) * half_rows
+                part[strip, g, side, at : at + half_rows, :] = value.astype(BF16)
+
+    def emit_and_send(strip, side):
         for d in range(groups - 1, 0, -1):
-            emit_for(lax.rem(group + d, groups))
-            part_copy(strip, d).start()
-        emit_for(group)
-
-    def summed(strip):
+            emit_for(strip, side, lax.rem(group + d, groups))
+            part_copy(strip, d, side).start()
+
+    def summed(strip, side):
         for d in range(1, groups):
-            part_copy(strip, d).wait_recv()
-        total = part[strip, group].astype(F32)
+            part_copy(strip, d, side).wait_recv()
+        total = part[strip, group, side].astype(F32)
         for d in range(1, groups):
-            total = total + got_part[strip, d - 1].astype(F32)
+            total = total + got_part[strip, d - 1, side].astype(F32)
         return total
 
     for copy in fetches[2:6]:
@@ -417,22 +417,30 @@
         return c
 
     lax.fori_loop(0, half + 2, slot, 0)
-    emit_strip(FAR)
+    for side in range(2):
+        emit_and_send(FAR, side)
+        emit_for(FAR, side, group)
     lax.fori_loop(half + 2, n, slot, 0)
+    emit_and_send(NEAR, 0)
     multiply(chunks - 1)
     turn(NEAR, chunks - 2)
     turn(NEAR, chunks - 1)
-    emit_strip(NEAR)
-
-    far_out[...] = summed(FAR).astype(BF16)
+    emit_and_send(NEAR, 1)
+
+    for side in range(2):
+        far_out[side] = summed(FAR, side).astype(BF16)
     cross = remote(far_out, far_in, far_sends.at[0], far_recvs.at[0], {"tile": far_tile})
     cross.start()
-    total = summed(NEAR)
+    for side in range(2):
+        emit_for(NEAR, side, group)
+    totals = [summed(NEAR, side) for side in range(2)]
     cross.wait_recv()
-    total = total + far_in[...].astype(F32)
+    totals = [totals[side] + far_in[side].astype(F32) for side in range(2)]
     tall = rows + 16
     for i in range(2 * blocks):
-        first[tall * i + 8 : tall * i + 8 + rows, :] = total[i * rows : (i + 1) * rows]
+        for side in range(2):
+            at = tall * i + 8 + side * half_rows
+            first[at : at + half_rows, :] = totals[side][i * half_rows : (i + 1) * half_rows]
     for i in range(HALO):
         halo_out[1, i, 0 : 2 * blocks, :] = first[pl.ds(8 + i, 2 * blocks, stride=tall), :]
         halo_out[0, i, 0 : 2 * blocks, :] = first[
@@ -550,7 +558,8 @@
     cross.wait_send()
     for strip in (NEAR, FAR):
         for d in range(1, groups):
-            part_copy(strip, d).wait_send()
+            for side in range(2):
+                part_copy(strip, d, side).wait_send()
 
 
 def body(echoes, pulse_slope, pulse_shift, footprint, band_start, row_phase):
@@ -570,7 +579,7 @@
     edge_rows = 8 * (-(-2 * blocks // 8))
     value_rows = 8 * (-(-held * planes // 8))
     field = (2 * blocks * (rows + 16), 128)
-    piece = (2 * blocks * rows, 128)
+    piece = (2, blocks * rows, 128)
     dma = pltpu.SemaphoreType.DMA
     refined = pl.pallas_call(
         functools.partial(kernel, held, pulses, rows, groups, n),
@@ -610,8 +619,8 @@
             dma((n // 2,)),
             dma((n // 2,)),
             dma((n // 2,)),
-            dma((2, groups - 1)),
-            dma((2, groups - 1)),
+            dma((2, groups - 1, 2)),
+            dma((2, groups - 1, 2)),
             dma((1,)),
             dma((1,)),
             dma((2,)),

time: 45.9 us -> 46.6 us (1.015)
  Pallas kernels: 42.2 us -> 42.9 us
    pallas_call x1, Pallas kernels: 42.2 us -> 42.9 us  [body(): pl.pallas_call(functools.partial(kernel, held, pulses, rows, groups, n),...]
where the time goes in v7:
time: 46.6 us; the launch traced here: 46.4 us
  Pallas kernels  42.9 us (92%)
  local copies, waits for them, and re-layouts  3.53 us (8%)
    pallas_call x1, Pallas kernels, body(): pl.pallas_call(functools.partial(kernel, held, pulses, rows, groups, n),...  42.9 us
    reshape x1, local copies, waits for them, and re-layouts, body(): planes_of = echoes.reshape(held, planes * bins, 128)  1.85 us
    unnamed x1, local copies, waits for them, and re-layouts  1.67 us

profile of v7, /device:TPU:0, one launch (start us, length us, event | category | flops | bytes accessed | tf_op | source)
XLA Modules:
  0.0 46.4 jit_solution(16155105446369902451)
XLA Ops:
  0.0 1.9 %reshape.10.echo_hbm = bf16[2,512,128]{2,1,0:T(8,128)(2,1)} reshape(bf16[2,2,2,16384]{3,2,1,0:T(2,128)(2,1)} %param.7) | data formatting | bytes 524288 | tf_op jit(solution)/shard_map/reshape | solution.py:573
  1.9 42.9 %shard_map.73 = f32[2,32,1024]{2,1,0:T(8,128)} custom-call(s32[1,8,8]{2,1,0:T(8,128)} %lists_hbm.1, s32[1,32]{1,0:T(1,128)} %bitcast.2, bf16[2,512,128]{2,1,0:T(8,128)(2,1)} %reshape.10.echo_hbm, bf16[2,2]{1,0:T(2,128)(2,1)} %slope_hbm.1, bf16[2,2]{1,0:T(2,128)(2,1)} %shift_hbm.1, f32[1,32]{1,0:T(1,128)} %bitcast.3, bf16[512,512]{1,0:T(8,128)(2,1)} %constant.2.clone.table_hbm), custom_call_target="tpu_custom_call" | custom-call | tf_op jit(solution)/shard_map/pallas_call | solution.py:584
  44.8 1.7 %copy.9 = f32[2,32,1024]{2,1,0:T(8,128)} copy(f32[2,32,1024]{2,1,0:T(8,128)} %shard_map.73) | data formatting | bytes 524288
